TPU v7x, 32 devices: a whole 2x2x4 slice. The times are simulated.
32 devices in a mesh: ctx: 4 (over y, x), exp: 8 (over z, core).
Axes of the slice: x: 2, y: 2, z: 4, core: 2. Of those that a mesh axis runs over, the one named last changes fastest.
Arguments:
- query_heads: bfloat16 [1024, 8, 128], P('ctx', 'exp'), may hold values from -0.59765625 to 0.59765625
- key_heads: bfloat16 [1024, 8, 128], P('ctx', 'exp'), may hold values from -0.59765625 to 0.59765625
- value_heads: bfloat16 [1024, 8, 128], P('ctx', 'exp'), may hold values from -6 to 6
- out_grad: bfloat16 [1024, 8, 128], P('ctx', 'exp'), may hold values from -0.29882812 to 0.29882812
- log_decay: bfloat16 [1024, 8, 128], P('ctx', 'exp'), may hold values from -1 to 0, as said below
- start_state: float32 [4, 8, 128, 128], P('ctx', 'exp'), may hold values from -24 to 24
- layer_grad: bfloat16 [1024, 2304], P(('ctx', 'exp')), may hold values from -6 to 6
- gate_weights: float32 [1024, 8], P(('ctx', 'exp')), may hold values from 0.1 to 1
- routes: int32 [1024, 8], P(('ctx', 'exp')), may hold values from 0 to 31, all different within a row; in each aligned block of 32 rows (0 to 31, 32 to 63, ...) at most 16 rows name the same one
- expert_down: bfloat16 [32, 512, 2304], P('exp'), may hold values from -0.125 to 0.125
Outputs:
- query_grad: bfloat16 [1024, 8, 128], P('ctx', 'exp')
- key_grad: bfloat16 [1024, 8, 128], P('ctx', 'exp')
- value_grad: bfloat16 [1024, 8, 128], P('ctx', 'exp')
- hidden_grad: bfloat16 [4, 8, 32, 16, 512], P('ctx', None, 'exp')
Inputs may be any that keep to these rules, and one draw needn't show every extreme that they name: `routes`: each row names 8 different experts. Within the 32 rows of one device no expert is named by more than 16 rows, a bound that some block reaches. `log_decay`: every entry is at most zero.
All inputs are finite; a program needn't handle non-finite values.
Results may differ from a plain program's by a relative error of at most 0.0049.
Values may be sent and summed in bfloat16 or wider, within the bound.
A program may use at most 64 MiB of HBM per device.

v0:
```python
import jax
import jax.numpy as jnp
from jax import lax
from jax.sharding import PartitionSpec as P

EXPERTS = 32
MOST = 16


BEST_MATMUL_MODE = lax.Precision.HIGHEST


def shifted(shard, axis, by):
    peers = lax.axis_size(axis)
    pairs = [(i, i + by) for i in range(peers) if 0 <= i + by < peers]
    return lax.ppermute(shard, axis, pairs)


def contraction_dimension_pairs(form, left, right):
    return jnp.einsum(
        form, left, right, precision=BEST_MATMUL_MODE, preferred_element_type=jnp.float32
    )


def advance(running_state, item):
    factor, addition = item
    return (factor[:, None] * running_state + addition, running_state)


def retreat(carried, item):
    factor, addition = item
    return (addition + factor[:, None] * carried, carried)


def local(
    query_heads,
    key_heads,
    value_heads,
    out_grad,
    log_decay,
    start_state,
    layer_grad,
    gate_weights,
    routes,
    expert_down,
):
    length = query_heads.shape[0]
    width = min(64, length)
    count = length // width
    queries = query_heads[:, 0, :].astype(jnp.float32).reshape(count, width, -1)
    key_rows = key_heads[:, 0, :].astype(jnp.float32).reshape(count, width, -1)
    value_row_list = value_heads[:, 0, :].astype(jnp.float32).reshape(count, width, -1)
    gradient_rows = out_grad[:, 0, :].astype(jnp.float32).reshape(count, width, -1)
    decays = log_decay[:, 0, :].astype(jnp.float32).reshape(count, width, -1)
    places = lax.iota(jnp.int32, width)
    lower = (places[:, None] >= places[None, :]).astype(jnp.float32)
    cumulative = contraction_dimension_pairs("ts,nsk->ntk", lower, decays)
    block_ends = cumulative[:, -1, :]
    enlarged = queries * jnp.exp(cumulative)
    reduced = key_rows * jnp.exp(-cumulative)
    tail_scale = jnp.exp(block_ends[:, None, :] - cumulative)
    trailing_key_rows = key_rows * tail_scale
    local_summands = contraction_dimension_pairs("loc,loh->lch", enlarged, gradient_rows)
    offsets = jnp.cumsum(block_ends, axis=0) - block_ends
    message = jnp.sum(jnp.exp(offsets)[:, :, None] * local_summands, axis=0)
    whole_decay = jnp.exp(jnp.sum(block_ends, axis=0))
    end_factor = jnp.exp(block_ends)
    partial_terms = contraction_dimension_pairs("ldr,ldo->lro", trailing_key_rows, value_row_list)
    unused_state, start_times = lax.scan(advance, start_state[0, 0], (end_factor, partial_terms))

    def relay(number, received):
        outgoing = message + whole_decay[:, None] * received
        return shifted(outgoing, "ctx", -1)

    incoming = lax.fori_loop(0, lax.axis_size("ctx") - 1, relay, jnp.zeros_like(message))
    unused_carry, arrival_times = lax.scan(
        retreat, incoming, (end_factor, local_summands), reverse=True
    )
    score_matrix = (
        contraction_dimension_pairs("ntv,nsv->nts", gradient_rows, value_row_list) * lower
    )
    affinity = contraction_dimension_pairs("nuk,ntk->nut", enlarged, reduced) * lower
    query_grad = jnp.exp(cumulative) * (
        contraction_dimension_pairs("ruo,rho->ruh", gradient_rows, start_times)
        + contraction_dimension_pairs("agc,acw->agw", score_matrix, reduced)
    )
    key_grad = jnp.exp(-cumulative) * contraction_dimension_pairs(
        "nst,nsk->ntk", score_matrix, enlarged
    ) + tail_scale * contraction_dimension_pairs("ruo,rho->ruh", value_row_list, arrival_times)
    value_grad = contraction_dimension_pairs(
        "nut,nuv->ntv", affinity, gradient_rows
    ) + contraction_dimension_pairs("jox,jxa->joa", trailing_key_rows, arrival_times)
    model_width = layer_grad.shape[1]
    local_count = expert_down.shape[0]
    flat_routes = routes.reshape(-1)
    indicator_matrix = (flat_routes[:, None] == lax.iota(jnp.int32, EXPERTS)[None, :]).astype(
        jnp.int32
    )
    before = jnp.cumsum(indicator_matrix, axis=0) - indicator_matrix
    position = flat_routes * MOST + jnp.sum(before * indicator_matrix, axis=1)
    scaled = (
        (gate_weights[:, :, None] * layer_grad[:, None, :].astype(jnp.float32))
        .astype(jnp.bfloat16)
        .reshape(-1, model_width)
    )
    buffer = (
        jnp.zeros((EXPERTS * MOST, model_width), jnp.bfloat16)
        .at[position]
        .set(scaled)
        .reshape(EXPERTS, MOST, model_width)
    )
    received = lax.all_to_all(buffer, "exp", split_axis=0, concat_axis=0, tiled=True)
    senders = received.shape[0] // local_count
    shaped = received.reshape(senders, local_count, received.shape[1], received.shape[2])
    product = jnp.einsum(
        "slmd,lfd->slmf", shaped, expert_down, preferred_element_type=jnp.float32
    ).astype(jnp.bfloat16)
    hidden = product.reshape(senders * local_count, received.shape[1], product.shape[3])
    hidden_grad = hidden.reshape(
        1, hidden.shape[0] // local_count, local_count, hidden.shape[1], hidden.shape[2]
    )
    return (
        query_grad.reshape(length, 1, -1).astype(jnp.bfloat16),
        key_grad.reshape(length, 1, -1).astype(jnp.bfloat16),
        value_grad.reshape(length, 1, -1).astype(jnp.bfloat16),
        hidden_grad,
    )


def solution(mesh):
    return jax.shard_map(
        local,
        mesh=mesh,
        in_specs=(
            P("ctx", "exp", None),
            P("ctx", "exp", None),
            P("ctx", "exp", None),
            P("ctx", "exp", None),
            P("ctx", "exp", None),
            P("ctx", "exp", None, None),
            P(("ctx", "exp"), None),
            P(("ctx", "exp"), None),
            P(("ctx", "exp"), None),
            P("exp", None, None),
        ),
        out_specs=(
            P("ctx", "exp", None),
            P("ctx", "exp", None),
            P("ctx", "exp", None),
            P("ctx", None, "exp", None, None),
        ),
        check_vma=False,
    )
```

profile of v0, /device:TPU:0, one launch (start us, length us, event | category | flops | bytes accessed | tf_op | source)
XLA Modules:
  0.0 78.1 jit_solution(11535251323000269420)
XLA Ops:
  0.6 0.7 broadcast_multiply_fusion
  1.4 0.8 copy.20
  2.5 0.8 copy.23
  3.3 0.6 reduce-window.6
  4.2 0.9 %convert_element_type.102 = f32[32,2304]{1,0:T(8,128)S(1)} convert(bf16[32,2304]{1,0:T(8,128)(2,1)} %param.22) | non-fusion elementwise | flops 73728 | bytes 442368 | tf_op jit(solution)/shard_map/convert_element_type | solution.py:102
  5.2 4.1 %scatter_custom_fusion = bf16[512,2304]{1,0:T(8,128)(2,1)} fusion(s32[256]{0:T(256)S(1)} %bitcast.139, f32[32,2304]{1,0:T(8,128)S(1)} %convert_element_type.102, f32[256]{0:T(256)S(1)} %mul.140, bf16[]{:T(256)} %constant.68.clone.1), kind=kCustom, calls=%fused_computation.17 | custom fusion | flops 1179648 | bytes 2655234 | tf_op jit(solution)/shard_map/scatter | solution.py:109
  9.3 6.5 %all-to-all-start = ((bf16[32,16,2304]{2,1,0:T(8,128)(2,1)}), bf16[32,16,2304]{2,1,0:T(8,128)(2,1)S(1)}, u32[]{:S(2)}, u32[]{:S(2)}) async-start(bf16[32,16,2304]{2,1,0:T(8,128)(2,1)} %bitcast.25), calls=%async_computation | async-start | bytes 4718592 | tf_op jit(solution)/shard_map/all_to_all | solution.py:112
  16.6 1.0 %convolution_multiply_fusion.2 = f32[4,64,128]{2,1,0:T(8,128)} fusion(f32[4,64,64]{2,1,0:T(8,128)S(1)} %convolution_multiply_fusion, f32[4,64,128]{2,1,0:T(8,128)S(1)} %convolution_bitcast_fusion.2, bf16[4,64,128]{2,1,0:T(8,128)(2,1)S(1)} %bitcast.124), kind=kOutput, calls=%fused_computation.30 | convolution fusion | flops 25296896 | bytes 393216 | tf_op jit(solution)/shard_map/nst,nsk->ntk/dot_general | solution.py:20
  17.6 0.9 %fusion.29 = f32[4,64,128]{2,1,0:T(8,128)} fusion(f32[4,64,64]{2,1,0:T(8,128)S(1)} %convolution_multiply_fusion, bf16[4,64,128]{2,1,0:T(8,128)(2,1)S(1)} %bitcast.120, f32[4,64,128]{2,1,0:T(8,128)S(1)} %convolution_bitcast_fusion.2), kind=kOutput, calls=%fused_computation.42 | convolution fusion | flops 25264128 | bytes 393216 | tf_op jit(solution)/shard_map/agc,acw->agw/dot_general | solution.py:20
  19.6 0.9 %fusion.40 = f32[4,64,128]{2,1,0:T(8,128)} fusion(f32[4,64,64]{2,1,0:T(8,128)S(1)} %convolution_multiply_fusion.1, bf16[4,64,128]{2,1,0:T(8,128)(2,1)S(1)} %bitcast.116), kind=kOutput, calls=%fused_computation.62 | convolution fusion | flops 25165824 | bytes 262144 | tf_op jit(solution)/shard_map/nut,nuv->ntv/dot_general | solution.py:20
  21.0 1.9 %fusion.26 = bf16[4,64,128]{2,1,0:T(8,128)(2,1)} fusion(f32[4,64,128]{2,1,0:T(8,128)} %fusion.29, f32[4,128,128]{2,1,0:T(8,128)S(1)} %get-tuple-element.156, bf16[4,64,128]{2,1,0:T(8,128)(2,1)S(1)} %bitcast.113, f32[4,64,128]{2,1,0:T(8,128)S(1)} %convolution_bitcast_fusion.2), kind=kOutput, calls=%fused_computation.33 | convolution fusion | flops 50429952 | bytes 655360 | tf_op jit(solution)/shard_map/ruo,rho->ruh/dot_general | solution.py:20
  22.9 20.2 %while.39 = (s32[]{:T(128)}, f32[128,128]{1,0:T(8,128)S(1)}, f32[128]{0:T(128)S(1)}, f32[128,128]{1,0:T(8,128)S(1)}, s32[]{:T(128)}) while((s32[]{:T(128)}, f32[128,128]{1,0:T(8,128)S(1)}, f32[128]{0:T(128)S(1)}, f32[128,128]{1,0:T(8,128)S(1)}, s32[]{:T(128)}) %tuple.72), condition=%wide.region_6.7_spmd, body=%wide.region_5.6_spmd.sunk | while | flops 32770 | bytes 459365 | solution.py:75
  23.0 1.3 %collective-permute-start = (f32[128,128]{1,0:T(8,128)S(1)}, f32[128,128]{1,0:T(8,128)S(1)}, u32[]{:S(2)}, u32[]{:S(2)}) collective-permute-start(f32[128,128]{1,0:T(8,128)S(1)} %multiply_add_fusion.2), channel_id=1, source_target_pairs={{8,0},{16,8},{24,16},{9,1},{17,9},{25,17},{10,2},{18,10},{26,18},{... | collective-permute-start | bytes 196616 | tf_op jit(solution)/shard_map/while/body/eval_jaxpr/ppermute | solution.py:16
  24.3 5.1 %collective-permute-done = f32[128,128]{1,0:T(8,128)S(1)} collective-permute-done((f32[128,128]{1,0:T(8,128)S(1)}, f32[128,128]{1,0:T(8,128)S(1)}, u32[]{:S(2)}, u32[]{:S(2)}) %collective-permute-start) | collective-permute-done | bytes 65568 | tf_op jit(solution)/shard_map/while/body/eval_jaxpr/ppermute | solution.py:16
  29.5 1.3 %collective-permute-start = (f32[128,128]{1,0:T(8,128)S(1)}, f32[128,128]{1,0:T(8,128)S(1)}, u32[]{:S(2)}, u32[]{:S(2)}) collective-permute-start(f32[128,128]{1,0:T(8,128)S(1)} %multiply_add_fusion.2), channel_id=1, source_target_pairs={{8,0},{16,8},{24,16},{9,1},{17,9},{25,17},{10,2},{18,10},{26,18},{... | collective-permute-start | bytes 196616 | tf_op jit(solution)/shard_map/while/body/eval_jaxpr/ppermute | solution.py:16
  30.8 5.2 %collective-permute-done = f32[128,128]{1,0:T(8,128)S(1)} collective-permute-done((f32[128,128]{1,0:T(8,128)S(1)}, f32[128,128]{1,0:T(8,128)S(1)}, u32[]{:S(2)}, u32[]{:S(2)}) %collective-permute-start) | collective-permute-done | bytes 65568 | tf_op jit(solution)/shard_map/while/body/eval_jaxpr/ppermute | solution.py:16
  36.1 1.3 %collective-permute-start = (f32[128,128]{1,0:T(8,128)S(1)}, f32[128,128]{1,0:T(8,128)S(1)}, u32[]{:S(2)}, u32[]{:S(2)}) collective-permute-start(f32[128,128]{1,0:T(8,128)S(1)} %multiply_add_fusion.2), channel_id=1, source_target_pairs={{8,0},{16,8},{24,16},{9,1},{17,9},{25,17},{10,2},{18,10},{26,18},{... | collective-permute-start | bytes 196616 | tf_op jit(solution)/shard_map/while/body/eval_jaxpr/ppermute | solution.py:16
  37.4 5.8 %collective-permute-done = f32[128,128]{1,0:T(8,128)S(1)} collective-permute-done((f32[128,128]{1,0:T(8,128)S(1)}, f32[128,128]{1,0:T(8,128)S(1)}, u32[]{:S(2)}, u32[]{:S(2)}) %collective-permute-start) | collective-permute-done | bytes 65568 | tf_op jit(solution)/shard_map/while/body/eval_jaxpr/ppermute | solution.py:16
  43.2 0.6 while.40
  43.7 2.0 %fusion.25 = bf16[4,64,128]{2,1,0:T(8,128)(2,1)} fusion(f32[4,64,128]{2,1,0:T(8,128)} %convolution_multiply_fusion.2, f32[4,128,128]{2,1,0:T(8,128)S(1)} %get-tuple-element.158, bf16[4,64,128]{2,1,0:T(8,128)(2,1)} %bitcast.126, f32[4,64,128]{2,1,0:T(8,128)S(1)} %convolution_bitcast_fusion.2, f32[4,128]{1,0:T(4,128)S(1)} %bitcast.132), kind=kOutput, calls=%fused_computation.32 | convolution fusion | flops 50462720 | bytes 657408 | tf_op jit(solution)/shard_map/ruo,rho->ruh/dot_general | solution.py:20
  45.7 1.9 %fusion.27 = bf16[4,64,128]{2,1,0:T(8,128)(2,1)} fusion(f32[4,64,128]{2,1,0:T(8,128)} %fusion.40, f32[4,128,128]{2,1,0:T(8,128)S(1)} %get-tuple-element.158, bf16[4,64,128]{2,1,0:T(8,128)(2,1)S(1)} %bitcast.122, f32[4,64,128]{2,1,0:T(8,128)S(1)} %convolution_bitcast_fusion.2, f32[4,128]{1,0:T(4,128)S(1)} %bitcast.133), kind=kOutput, calls=%fused_computation.34 | convolution fusion | flops 50495488 | bytes 657408 | tf_op jit(solution)/shard_map/jox,jxa->joa/dot_general | solution.py:20
  47.6 22.9 %all-to-all-done = bf16[32,16,2304]{2,1,0:T(8,128)(2,1)S(1)} async-done(((bf16[32,16,2304]{2,1,0:T(8,128)(2,1)}), bf16[32,16,2304]{2,1,0:T(8,128)(2,1)S(1)}, u32[]{:S(2)}, u32[]{:S(2)}) %all-to-all-start) | async-done | bytes 2359328 | tf_op jit(solution)/shard_map/all_to_all | solution.py:112
  70.5 6.8 %fusion.11 = bf16[1,8,4,16,512]{4,3,1,2,0:T(8,128)(2,1)S(1)} fusion(bf16[4,512,2304]{2,1,0:T(8,128)(2,1)} %param.25, bf16[8,4,16,2304]{3,2,1,0:T(8,128)(2,1)S(1)} %bitcast.117), kind=kOutput, calls=%fused_computation.16 | convolution fusion | flops 1208221696 | bytes 12320768 | tf_op jit(solution)/shard_map/slmd,lfd->slmf/dot_general | solution.py:115
  77.3 0.8 %copy.25 = bf16[1,8,4,16,512]{4,3,2,1,0:T(8,128)(2,1)} copy(bf16[1,8,4,16,512]{4,3,1,2,0:T(8,128)(2,1)S(1)} %fusion.11) | data formatting | bytes 1048576
  (64 shorter events, 4.1 us)
Async XLA Ops:
  0.6 15.4 %copy-start = (bf16[256,1,128]{2,0,1:T(8,128)(2,1)S(1)}, bf16[256,1,128]{2,0,1:T(8,128)(2,1)}, u32[]{:S(2)}) copy-start(bf16[256,1,128]{2,0,1:T(8,128)(2,1)} %param.19) | copy-start | bytes 196612
  9.3 6.5 %copy-start.5 = (bf16[256,1,128]{2,0,1:T(8,128)(2,1)S(1)}, bf16[256,1,128]{2,0,1:T(8,128)(2,1)}, u32[]{:S(2)}) copy-start(bf16[256,1,128]{2,0,1:T(8,128)(2,1)} %param.20) | copy-start | bytes 196612
  9.3 6.7 %copy-start.4 = (bf16[256,1,128]{2,0,1:T(8,128)(2,1)S(1)}, bf16[256,1,128]{2,0,1:T(8,128)(2,1)}, u32[]{:S(2)}) copy-start(bf16[256,1,128]{2,0,1:T(8,128)(2,1)} %param.18) | copy-start | bytes 196612
  9.3 6.9 %copy-start.2 = (bf16[256,1,128]{2,0,1:T(8,128)(2,1)S(1)}, bf16[256,1,128]{2,0,1:T(8,128)(2,1)}, u32[]{:S(2)}) copy-start(bf16[256,1,128]{2,0,1:T(8,128)(2,1)} %param.17) | copy-start | bytes 196612
  9.3 6.9 %copy-start.3 = (bf16[256,1,128]{2,0,1:T(8,128)(2,1)S(1)}, bf16[256,1,128]{2,0,1:T(8,128)(2,1)}, u32[]{:S(2)}) copy-start(bf16[256,1,128]{2,0,1:T(8,128)(2,1)} %param.16) | copy-start | bytes 196612
  9.3 61.2 %all-to-all-start = ((bf16[32,16,2304]{2,1,0:T(8,128)(2,1)}), bf16[32,16,2304]{2,1,0:T(8,128)(2,1)S(1)}, u32[]{:S(2)}, u32[]{:S(2)}) async-start(bf16[32,16,2304]{2,1,0:T(8,128)(2,1)} %bitcast.25), calls=%async_computation | async-start | bytes 4718592 | tf_op jit(solution)/shard_map/all_to_all | solution.py:112
  15.8 3.2 %copy-start.1 = (f32[1,1,128,128]{3,2,1,0:T(8,128)S(1)}, f32[1,1,128,128]{3,2,1,0:T(8,128)}, u32[]{:S(2)}) copy-start(f32[1,1,128,128]{3,2,1,0:T(8,128)} %param.21) | copy-start | bytes 196612
  23.0 6.4 %collective-permute-start = (f32[128,128]{1,0:T(8,128)S(1)}, f32[128,128]{1,0:T(8,128)S(1)}, u32[]{:S(2)}, u32[]{:S(2)}) collective-permute-start(f32[128,128]{1,0:T(8,128)S(1)} %multiply_add_fusion.2), channel_id=1, source_target_pairs={{8,0},{16,8},{24,16},{9,1},{17,9},{25,17},{10,2},{18,10},{26,18},{... | collective-permute-start | bytes 196616 | tf_op jit(solution)/shard_map/while/body/eval_jaxpr/ppermute | solution.py:16
  29.5 6.5 %collective-permute-start = (f32[128,128]{1,0:T(8,128)S(1)}, f32[128,128]{1,0:T(8,128)S(1)}, u32[]{:S(2)}, u32[]{:S(2)}) collective-permute-start(f32[128,128]{1,0:T(8,128)S(1)} %multiply_add_fusion.2), channel_id=1, source_target_pairs={{8,0},{16,8},{24,16},{9,1},{17,9},{25,17},{10,2},{18,10},{26,18},{... | collective-permute-start | bytes 196616 | tf_op jit(solution)/shard_map/while/body/eval_jaxpr/ppermute | solution.py:16
  36.1 7.1 %collective-permute-start = (f32[128,128]{1,0:T(8,128)S(1)}, f32[128,128]{1,0:T(8,128)S(1)}, u32[]{:S(2)}, u32[]{:S(2)}) collective-permute-start(f32[128,128]{1,0:T(8,128)S(1)} %multiply_add_fusion.2), channel_id=1, source_target_pairs={{8,0},{16,8},{24,16},{9,1},{17,9},{25,17},{10,2},{18,10},{26,18},{... | collective-permute-start | bytes 196616 | tf_op jit(solution)/shard_map/while/body/eval_jaxpr/ppermute | solution.py:16
where the time goes:
time: 78.6 us; the launch traced here: 78.1 us
  waiting for transfers between devices  38.9 us (49%)
  matrix products  17 us (22%)
  starting transfers between devices  10.3 us (13%)
  other arithmetic  7.53 us (10%)
  local copies, waits for them, and re-layouts  3.22 us (4%)
  between operations  0.8 us (1%)
    all_to_all x1, waiting for transfers between devices, local(): lax.all_to_all(buffer, 'exp', split_axis=0, concat_axis=0, tiled=True)  22.9 us
    ppermute x3, waiting for transfers between devices, shifted(): return lax.ppermute(shard, axis, pairs)  16.1 us
    dot_general x11, matrix products, contraction_dimension_pairs(): jnp.einsum(form, left, right, precision=BEST_MATMUL_MODE, preferred_eleme...  10.2 us
    dot_general x1, matrix products, local(): jnp.einsum('slmd,lfd->slmf', shaped, expert_down, preferred_element_type=...  6.8 us
    all_to_all x1, starting transfers between devices, local(): lax.all_to_all(buffer, 'exp', split_axis=0, concat_axis=0, tiled=True)  6.47 us
    scatter x1, other arithmetic, local(): buffer = jnp.zeros((EXPERTS * MOST, model_width), jnp.bfloat16).at[positi...  4.09 us
    ppermute x3, starting transfers between devices, shifted(): return lax.ppermute(shard, axis, pairs)  3.88 us
    unnamed x15, local copies, waits for them, and re-layouts  2.4 us
  transfers between devices with their start and end apart: 4, of which 4 were waited for; matrix products, arithmetic and copies ran while one was open for 15% of the time, Pallas kernels for 0%

commit v1 on v0

v1 whole, which is shorter than its diff:
```python
import functools

import jax
import jax.numpy as jnp
from jax import lax
from jax.experimental import pallas as pl
from jax.experimental.pallas import tpu as pltpu
from jax.sharding import PartitionSpec as P

MOST = 16
F32 = jnp.float32
BF16 = jnp.bfloat16
MESH = pl.DeviceIdType.MESH


def dot(a, b, ca, cb):
    return lax.dot_general(a, b, (((ca,), (cb,)), ((), ())), preferred_element_type=F32)


def split(x):
    high = x.astype(BF16)
    return [high, (x - high.astype(F32)).astype(BF16)]


def mm(a, b, ca, cb):
    total = None
    for i, left in enumerate(a):
        for j, right in enumerate(b):
            if i + j < 2:
                term = dot(left, right, ca, cb)
                total = term if total is None else total + term
    return total


def kernel(
    groups, peers, chunk,
    q_hbm, k_hbm, v_hbm, g_hbm, d_hbm, s_hbm, x_hbm, gate_hbm, route_hbm, w_hbm,
    qg_hbm, kg_hbm, vg_hbm, out_hbm,
    q_ref, k_ref, v_ref, g_ref, d_ref, s_ref, gate_ref, route_ref, meta, xall, w_ref,
    pick, scale, slots, out_ref, qg_ref, kg_ref, vg_ref, message, arrived, carry, ed_ref, red_ref,
    kpart, vpart, mstate, lsem, wsem, osem, msend, mrecv, xown, xlocal, xsend, xrecv, csend, crecv,
):
    c = lax.axis_index("ctx")
    s = lax.axis_index("exp")
    z = s // 2
    h = s % 2
    line = peers // 2
    sibling = z * 2 + 1 - h
    length = q_ref.shape[0]
    count = length // chunk
    experts = w_ref.shape[0]
    tokens = xall.shape[1]

    barrier = pltpu.get_barrier_semaphore()
    for off in range(1, peers):
        pl.semaphore_signal(barrier, inc=1, device_id={"exp": (s + off) % peers}, device_id_type=MESH)
    for off in range(1, groups):
        pl.semaphore_signal(barrier, inc=1, device_id={"ctx": (c + off) % groups}, device_id_type=MESH)

    loads = [
        pltpu.make_async_copy(src, dst, lsem.at[i])
        for i, (src, dst) in enumerate([
            (gate_hbm, gate_ref), (route_hbm, route_ref), (d_hbm, d_ref), (q_hbm, q_ref), (g_hbm, g_ref),
            (k_hbm, k_ref), (v_hbm, v_ref), (s_hbm, s_ref),
        ])
    ]
    for load in loads:
        load.start()
    own = pltpu.make_async_copy(x_hbm, xall.at[s], xlocal)
    own.start()
    weights = [pltpu.make_async_copy(w_hbm.at[e], w_ref.at[e], wsem.at[e]) for e in range(experts)]
    for weight in weights:
        weight.start()
    loads[0].wait()
    loads[1].wait()
    top = gate_ref.shape[0]
    meta[s, 0:top] = gate_ref[...]
    meta[s, top:2 * top] = route_ref[...].astype(F32)

    pl.semaphore_wait(barrier, peers - 1 + groups - 1)

    def send_x(src, dst, slot, sem, to):
        return pltpu.make_async_remote_copy(
            src_ref=src, dst_ref=dst, send_sem=sem, recv_sem=xrecv.at[slot], device_id={"exp": to}, device_id_type=MESH
        )

    to_right = send_x(x_hbm, xall.at[s], s, xown.at[0], (s + 2) % peers)
    to_left = send_x(x_hbm, xall.at[s], s, xown.at[1], (s + peers - 2) % peers)
    to_sibling = send_x(x_hbm, xall.at[s], s, xown.at[2], sibling)

    @pl.when(z + 1 < line)
    def _():
        to_right.start()

    @pl.when(z >= 1)
    def _():
        to_left.start()

    to_sibling.start()

    metas = []
    for off in range(1, peers):
        metas.append(pltpu.make_async_remote_copy(
            src_ref=meta.at[s], dst_ref=meta.at[s], send_sem=msend.at[off], recv_sem=mrecv.at[s],
            device_id={"exp": (s + off) % peers}, device_id_type=MESH,
        ))
        metas[-1].start()

    def ways(d):
        left = (s + peers - 2 * d) % peers
        right = (s + 2 * d) % peers
        return (
            (left, z >= d, (s + 2) % peers, z + 1 < line),
            (right, z + d < line, (s + peers - 2) % peers, z >= 1),
        )

    def forwards(d, side):
        src, valid, onward, goes = ways(d)[side]
        on = send_x(xall.at[src], xall.at[src], src, xsend.at[(d - 1) * 4 + side * 2], onward)
        across = send_x(xall.at[src], xall.at[src], src, xsend.at[(d - 1) * 4 + side * 2 + 1], sibling)
        return src, valid, goes, on, across

    def relay(d):
        for side in range(2):
            src, valid, goes, on, across = forwards(d, side)

            @pl.when(valid)
            def _():
                across.wait_recv()

                @pl.when(goes)
                def _():
                    on.start()

                across.start()

    for load in loads[2:]:
        load.wait()
    rows = lax.broadcasted_iota(jnp.int32, (chunk, chunk), 0)
    cols = lax.broadcasted_iota(jnp.int32, (chunk, chunk), 1)
    lower = rows >= cols
    ones = jnp.where(lower, 1.0, 0.0).astype(BF16)
    ends, halves, ups, enlarged = [], [], [], []
    for a in range(count):
        part = pl.ds(a * chunk, chunk)
        cum = dot(ones, d_ref[part, :], 1, 0)
        end = cum[chunk - 1:chunk, :]
        up = jnp.exp(cum - 0.5 * end)
        ends.append(end)
        halves.append(jnp.exp(0.5 * end))
        ups.append(up)
        enl = split(q_ref[part, :].astype(F32) * up)
        enlarged.append(enl)
        mstate[a] = mm([g_ref[part, :]], enl, 0, 0) * halves[a]
        down = jnp.exp(0.5 * end - cum)
        ed_ref[part, :] = down
        red_ref[part, :] = k_ref[part, :].astype(F32) * down
    total = mstate[count - 1]
    for a in reversed(range(count - 1)):
        total = mstate[a] + jnp.exp(ends[a]) * total
    whole = ends[0]
    for a in range(1, count):
        whole = whole + ends[a]
    keys = message.shape[1]
    message[0:message.shape[0] - 8, :] = total
    message[message.shape[0] - 8:, :] = jnp.broadcast_to(jnp.exp(whole), (8, keys))

    def group_copy(d):
        return pltpu.make_async_remote_copy(
            src_ref=message, dst_ref=arrived.at[d - 1], send_sem=csend.at[d - 1], recv_sem=crecv.at[d - 1],
            device_id={"ctx": (c + groups - d) % groups}, device_id_type=MESH,
        )

    for d in range(1, groups):
        @pl.when(c >= d)
        def _():
            group_copy(d).start()

    if line > 1:
        relay(1)

    state = s_ref[...].T
    for a in range(count):
        part = pl.ds(a * chunk, chunk)
        g = g_ref[part, :]
        v = v_ref[part, :]
        red = split(red_ref[part, :])
        score = split(jnp.where(lower, dot(g, v, 1, 1), 0.0))
        flipped = split(jnp.where(rows <= cols, dot(v, g, 1, 1), 0.0))
        affinity = split(jnp.where(rows <= cols, mm(red, enlarged[a], 1, 1), 0.0))
        qg = mm([g], split(state * halves[a]), 1, 0) + mm(score, red, 1, 0)
        qg_ref[part, :] = (ups[a] * qg).astype(BF16)
        kpart[part, :] = mm(flipped, enlarged[a], 1, 0)
        vpart[part, :] = mm(affinity, [g], 1, 0)
        if a + 1 < count:
            state = jnp.exp(ends[a]) * state + mm([v], red, 0, 0) * halves[a]
    outs = [pltpu.make_async_copy(qg_ref, qg_hbm, osem.at[0])]
    outs[0].start()

    before = jnp.where(
        lax.broadcasted_iota(jnp.int32, (tokens, tokens), 0) < lax.broadcasted_iota(jnp.int32, (tokens, tokens), 1), 1.0, 0.0
    ).astype(BF16)

    def prepare(off, unused):
        src = (s + off) % peers

        @pl.when(off > 0)
        def _():
            pltpu.make_async_remote_copy(
                src_ref=meta.at[src], dst_ref=meta.at[src], send_sem=msend.at[0], recv_sem=mrecv.at[src],
                device_id={"exp": sibling}, device_id_type=MESH,
            ).wait_recv()

        gates = meta[src, 0:top]
        routes = meta[src, top:2 * top]
        first = (s * experts).astype(F32)
        place = lax.broadcasted_iota(jnp.int32, (MOST, tokens), 0).astype(F32)
        for e in range(experts):
            hit = routes == first + e
            member = jnp.sum(jnp.where(hit, 1.0, 0.0), axis=0, keepdims=True)
            gate = jnp.sum(jnp.where(hit, gates, 0.0), axis=0, keepdims=True)
            earlier = dot(jnp.broadcast_to(member, (8, tokens)).astype(BF16), before, 1, 0)[0:1]
            chosen = jnp.where(
                (jnp.broadcast_to(member, (MOST, tokens)) > 0.5) & (jnp.broadcast_to(earlier, (MOST, tokens)) == place), 1.0, 0.0
            )
            pick[src, e * MOST:(e + 1) * MOST, :] = chosen.astype(BF16)
            scale[src, e * MOST:(e + 1) * MOST, :] = jnp.broadcast_to(
                jnp.sum(chosen * gate, axis=1, keepdims=True), (MOST, scale.shape[2])
            )
        return unused

    lax.fori_loop(0, peers, prepare, 0)

    def build(src):
        rows_of = dot(pick[src], xall[src], 1, 0)
        scaled = (rows_of * scale[src][:, 0:1]).astype(BF16)
        for e in range(experts):
            slots[e, pl.ds(pl.multiple_of(src * MOST, MOST), MOST), :] = scaled[e * MOST:(e + 1) * MOST]

    if line > 2:
        relay(2)
    own.wait()
    build(s)
    send_x(xall.at[sibling], xall.at[sibling], sibling, xown.at[2], sibling).wait_recv()
    build(sibling)

    def finish(d):
        def one(i, unused):
            side = i // 2
            across = i % 2
            step = jnp.where(side == 0, peers - 2 * d, 2 * d)
            valid = jnp.where(side == 0, z >= d, z + d < line)
            mine = (s + step) % peers
            other = (mine // 2) * 2 + 1 - h
            src = jnp.where(across == 0, mine, other)

            @pl.when(valid)
            def _():
                @pl.when(across == 1)
                def _():
                    send_x(xall.at[src], xall.at[src], src, xown.at[2], sibling).wait_recv()

                build(src)

            return unused

        lax.fori_loop(0, 4, one, 0)

    if line > 1:
        finish(1)

    carry[...] = jnp.zeros_like(carry)
    for d in reversed(range(1, groups)):
        @pl.when(c + d < groups)
        def _():
            group_copy(d).wait_recv()
            size = carry.shape[0]
            carry[...] = arrived[d - 1, 0:size, :] + arrived[d - 1, size:size + 1, :] * carry[...]
    after = carry[...]
    for a in reversed(range(count)):
        part = pl.ds(a * chunk, chunk)
        later = split(after * halves[a])
        kg = kpart[part, :] + mm([v_ref[part, :]], later, 1, 0)
        kg_ref[part, :] = (ed_ref[part, :] * kg).astype(BF16)
        vg = vpart[part, :] + mm(split(red_ref[part, :]), later, 1, 1)
        vg_ref[part, :] = vg.astype(BF16)
        if a > 0:
            after = mstate[a] + jnp.exp(ends[a]) * after
    outs.append(pltpu.make_async_copy(kg_ref, kg_hbm, osem.at[1]))
    outs.append(pltpu.make_async_copy(vg_ref, vg_hbm, osem.at[2]))
    outs[1].start()
    outs[2].start()

    for d in range(2, line):
        if d > 2:
            relay(d)
        finish(d)

    for e in range(experts):
        weights[e].wait()
        product = dot(slots[e], w_ref[e], 1, 1).astype(BF16)
        for src in range(peers):
            out_ref[src, e] = product[src * MOST:(src + 1) * MOST]
        outs.append(pltpu.make_async_copy(out_ref.at[:, e], out_hbm.at[0, :, e], osem.at[3 + e]))
        outs[-1].start()

    @pl.when(z + 1 < line)
    def _():
        to_right.wait_send()

    @pl.when(z >= 1)
    def _():
        to_left.wait_send()

    to_sibling.wait_send()
    for copy in metas:
        copy.wait_send()
    for d in range(1, line):
        for side in range(2):
            src, valid, goes, on, across = forwards(d, side)

            @pl.when(valid)
            def _():
                @pl.when(goes)
                def _():
                    on.wait_send()

                across.wait_send()
    for d in range(1, groups):
        @pl.when(c >= d)
        def _():
            group_copy(d).wait_send()
    for copy in outs:
        copy.wait()


def local(
    query_heads, key_heads, value_heads, out_grad, log_decay, start_state, layer_grad, gate_weights, routes, expert_down
):
    groups = lax.axis_size("ctx")
    peers = lax.axis_size("exp")
    length, heads, keys = query_heads.shape
    values = value_heads.shape[2]
    tokens, width = layer_grad.shape
    top = routes.shape[1]
    experts, hidden, _ = expert_down.shape
    chunk = min(128, length)
    count = length // chunk
    line = peers // 2
    dma = pltpu.SemaphoreType.DMA
    hbm = pl.BlockSpec(memory_space=pl.ANY)
    qg, kg, vg, out = pl.pallas_call(
        functools.partial(kernel, groups, peers, chunk),
        out_shape=(
            jax.ShapeDtypeStruct((length, keys), BF16),
            jax.ShapeDtypeStruct((length, keys), BF16),
            jax.ShapeDtypeStruct((length, values), BF16),
            jax.ShapeDtypeStruct((1, peers, experts, MOST, hidden), BF16),
        ),
        in_specs=[hbm] * 10,
        out_specs=(hbm,) * 4,
        scratch_shapes=[
            pltpu.VMEM((length, keys), BF16),
            pltpu.VMEM((length, keys), BF16),
            pltpu.VMEM((length, values), BF16),
            pltpu.VMEM((length, values), BF16),
            pltpu.VMEM((length, keys), BF16),
            pltpu.VMEM((keys, values), F32),
            pltpu.VMEM((top, tokens), F32),
            pltpu.VMEM((top, tokens), jnp.int32),
            pltpu.VMEM((peers, 2 * top, tokens), F32),
            pltpu.VMEM((peers, tokens, width), BF16),
            pltpu.VMEM((experts, hidden, width), BF16),
            pltpu.VMEM((peers, experts * MOST, tokens), BF16),
            pltpu.VMEM((peers, experts * MOST, 128), F32),
            pltpu.VMEM((experts, peers * MOST, width), BF16),
            pltpu.VMEM((peers, experts, MOST, hidden), BF16),
            pltpu.VMEM((length, keys), BF16),
            pltpu.VMEM((length, keys), BF16),
            pltpu.VMEM((length, values), BF16),
            pltpu.VMEM((values + 8, keys), F32),
            pltpu.VMEM((max(1, groups - 1), values + 8, keys), F32),
            pltpu.VMEM((values, keys), F32),
            pltpu.VMEM((length, keys), F32),
            pltpu.VMEM((length, keys), F32),
            pltpu.VMEM((length, keys), F32),
            pltpu.VMEM((length, values), F32),
            pltpu.VMEM((count, values, keys), F32),
            dma((8,)),
            dma((experts,)),
            dma((3 + experts,)),
            dma((peers,)),
            dma((peers,)),
            dma((3,)),
            dma,
            dma((max(1, line - 1) * 4,)),
            dma((peers,)),
            dma((max(1, groups - 1),)),
            dma((max(1, groups - 1),)),
        ],
        compiler_params=pltpu.CompilerParams(
            collective_id=0, has_side_effects=True, vmem_limit_bytes=56 * 1024 * 1024
        ),
        cost_estimate=pl.CostEstimate(
            flops=2 * experts * peers * MOST * width * hidden, bytes_accessed=2 * experts * width * hidden, transcendentals=0
        ),
    )(
        query_heads[:, 0, :],
        key_heads[:, 0, :],
        value_heads[:, 0, :],
        out_grad[:, 0, :],
        log_decay[:, 0, :],
        start_state[0, 0],
        layer_grad,
        gate_weights.T,
        routes.T,
        expert_down,
    )
    return (
        qg.reshape(length, heads, keys),
        kg.reshape(length, heads, keys),
        vg.reshape(length, heads, values),
        out,
    )


def solution(mesh):
    return jax.shard_map(
        local,
        mesh=mesh,
        in_specs=(
            P("ctx", "exp", None),
            P("ctx", "exp", None),
            P("ctx", "exp", None),
            P("ctx", "exp", None),
            P("ctx", "exp", None),
            P("ctx", "exp", None, None),
            P(("ctx", "exp"), None),
            P(("ctx", "exp"), None),
            P(("ctx", "exp"), None),
            P("exp", None, None),
        ),
        out_specs=(
            P("ctx", "exp", None),
            P("ctx", "exp", None),
            P("ctx", "exp", None),
            P("ctx", None, "exp", None, None),
        ),
        check_vma=False,
    )
```

time: 78.6 us -> 32.4 us (0.41)
  the two profiles are of different devices: /device:TPU:0 before, /device:TPU:1 now
where the time goes in v1:
time: 32.4 us; the launch traced here: 32.1 us
  Pallas kernels  25.2 us (78%)
  local copies, waits for them, and re-layouts  6.29 us (19%)
  between operations  0.64 us (2%)
    pallas_call x1, Pallas kernels, local(): pl.pallas_call(functools.partial(kernel, groups, peers, chunk), out_shape...  25.2 us
    unnamed x4, local copies, waits for them, and re-layouts  6.29 us

profile of v1, /device:TPU:1, one launch (start us, length us, event | category | flops | bytes accessed | tf_op | source)
XLA Modules:
  0.0 32.1 jit_solution(7074453971707035580)
XLA Ops:
  0.6 25.2 %shard_map.129 = (bf16[256,128]{1,0:T(8,128)(2,1)}, bf16[256,128]{1,0:T(8,128)(2,1)}, bf16[256,128]{1,0:T(8,128)(2,1)}, bf16[1,8,4,16,512]{4,3,2,1,0:T(8,128)(2,1)}) custom-call(bf16[256,128]{1,0:T(8,128)(2,1)} %bitcast.11, bf16[256,128]{1,0:T(8,128)(2,1)} %bitcast.12, bf16[256,128]{1,0:T(8,128)(2,1)} %bitcast.13, bf16[256,128]{1,0:T(8,128)(2,1)} %bitcast.14, ...), custom_call_target="tpu_custom_call" | custom-call | flops 1207959552 | bytes 9437184 | tf_op jit(solution)/shard_map/pallas_call | solution.py:352
  25.8 1.5 %copy.18 = bf16[256,1,128]{2,0,1:T(8,128)(2,1)} copy(bf16[256,1,128]{2,0,1:T(8,128)(2,1)} %bitcast.19) | data formatting | bytes 131072
  27.3 1.5 %copy.19 = bf16[256,1,128]{2,0,1:T(8,128)(2,1)} copy(bf16[256,1,128]{2,0,1:T(8,128)(2,1)} %bitcast.18) | data formatting | bytes 131072
  28.8 1.5 %copy.20 = bf16[256,1,128]{2,0,1:T(8,128)(2,1)} copy(bf16[256,1,128]{2,0,1:T(8,128)(2,1)} %bitcast.17) | data formatting | bytes 131072
  30.3 1.9 %copy.21 = bf16[1,8,4,16,512]{4,3,2,1,0:T(8,128)(2,1)} copy(bf16[1,8,4,16,512]{4,3,2,1,0:T(8,128)(2,1)} %get-tuple-element.19) | data formatting | bytes 1048576

commit v2 on v1

--- a/solution.py
+++ b/solution.py
@@ -35,10 +35,10 @@
 def kernel(
     groups, peers, chunk,
     q_hbm, k_hbm, v_hbm, g_hbm, d_hbm, s_hbm, x_hbm, gate_hbm, route_hbm, w_hbm,
-    qg_hbm, kg_hbm, vg_hbm, out_hbm,
+    qg_ref, kg_ref, vg_ref, out_ref,
     q_ref, k_ref, v_ref, g_ref, d_ref, s_ref, gate_ref, route_ref, meta, xall, w_ref,
-    pick, scale, slots, out_ref, qg_ref, kg_ref, vg_ref, message, arrived, carry, ed_ref, red_ref,
-    kpart, vpart, mstate, lsem, wsem, osem, msend, mrecv, xown, xlocal, xsend, xrecv, csend, crecv,
+    pick, scale, slots, message, arrived, carry, ed_ref, red_ref,
+    kpart, vpart, mstate, lsem, wsem, msend, mrecv, xown, xlocal, xsend, xrecv, csend, crecv,
 ):
     c = lax.axis_index("ctx")
     s = lax.axis_index("exp")
@@ -192,44 +192,34 @@
         qg_ref[part, :] = (ups[a] * qg).astype(BF16)
         kpart[part, :] = mm(flipped, enlarged[a], 1, 0)
         vpart[part, :] = mm(affinity, [g], 1, 0)
+        if a == 0 and line > 2:
+            relay(2)
         if a + 1 < count:
             state = jnp.exp(ends[a]) * state + mm([v], red, 0, 0) * halves[a]
-    outs = [pltpu.make_async_copy(qg_ref, qg_hbm, osem.at[0])]
-    outs[0].start()
 
     before = jnp.where(
         lax.broadcasted_iota(jnp.int32, (tokens, tokens), 0) < lax.broadcasted_iota(jnp.int32, (tokens, tokens), 1), 1.0, 0.0
     ).astype(BF16)
 
-    def prepare(off, unused):
+    for off in range(1, peers):
         src = (s + off) % peers
-
-        @pl.when(off > 0)
-        def _():
-            pltpu.make_async_remote_copy(
-                src_ref=meta.at[src], dst_ref=meta.at[src], send_sem=msend.at[0], recv_sem=mrecv.at[src],
-                device_id={"exp": sibling}, device_id_type=MESH,
-            ).wait_recv()
-
-        gates = meta[src, 0:top]
-        routes = meta[src, top:2 * top]
-        first = (s * experts).astype(F32)
-        place = lax.broadcasted_iota(jnp.int32, (MOST, tokens), 0).astype(F32)
-        for e in range(experts):
-            hit = routes == first + e
-            member = jnp.sum(jnp.where(hit, 1.0, 0.0), axis=0, keepdims=True)
-            gate = jnp.sum(jnp.where(hit, gates, 0.0), axis=0, keepdims=True)
-            earlier = dot(jnp.broadcast_to(member, (8, tokens)).astype(BF16), before, 1, 0)[0:1]
-            chosen = jnp.where(
-                (jnp.broadcast_to(member, (MOST, tokens)) > 0.5) & (jnp.broadcast_to(earlier, (MOST, tokens)) == place), 1.0, 0.0
-            )
-            pick[src, e * MOST:(e + 1) * MOST, :] = chosen.astype(BF16)
-            scale[src, e * MOST:(e + 1) * MOST, :] = jnp.broadcast_to(
-                jnp.sum(chosen * gate, axis=1, keepdims=True), (MOST, scale.shape[2])
-            )
-        return unused
-
-    lax.fori_loop(0, peers, prepare, 0)
+        pltpu.make_async_remote_copy(
+            src_ref=meta.at[src], dst_ref=meta.at[src], send_sem=msend.at[0], recv_sem=mrecv.at[src],
+            device_id={"exp": sibling}, device_id_type=MESH,
+        ).wait_recv()
+    gates = meta[:, 0:top]
+    routes = meta[:, top:2 * top]
+    first = (s * experts).astype(F32)
+    place = lax.broadcasted_iota(jnp.int32, (peers, MOST, tokens), 1).astype(F32)
+    for e in range(experts):
+        hit = routes == first + e
+        member = jnp.sum(jnp.where(hit, 1.0, 0.0), axis=1)
+        gate = jnp.sum(jnp.where(hit, gates, 0.0), axis=1)
+        earlier = jnp.where(member > 0.5, dot(member.astype(BF16), before, 1, 0), -1.0)
+        chosen = jnp.where(earlier[:, None, :] == place, 1.0, 0.0)
+        pick[:, e * MOST:(e + 1) * MOST, :] = chosen.astype(BF16)
+        weight = jnp.sum(chosen * gate[:, None, :], axis=2, keepdims=True)
+        scale[:, e * MOST:(e + 1) * MOST, :] = jnp.broadcast_to(weight, (peers, MOST, scale.shape[2]))
 
     def build(src):
         rows_of = dot(pick[src], xall[src], 1, 0)
@@ -237,8 +227,6 @@
         for e in range(experts):
             slots[e, pl.ds(pl.multiple_of(src * MOST, MOST), MOST), :] = scaled[e * MOST:(e + 1) * MOST]
 
-    if line > 2:
-        relay(2)
     own.wait()
     build(s)
     send_x(xall.at[sibling], xall.at[sibling], sibling, xown.at[2], sibling).wait_recv()
@@ -286,10 +274,6 @@
         vg_ref[part, :] = vg.astype(BF16)
         if a > 0:
             after = mstate[a] + jnp.exp(ends[a]) * after
-    outs.append(pltpu.make_async_copy(kg_ref, kg_hbm, osem.at[1]))
-    outs.append(pltpu.make_async_copy(vg_ref, vg_hbm, osem.at[2]))
-    outs[1].start()
-    outs[2].start()
 
     for d in range(2, line):
         if d > 2:
@@ -300,9 +284,7 @@
         weights[e].wait()
         product = dot(slots[e], w_ref[e], 1, 1).astype(BF16)
         for src in range(peers):
-            out_ref[src, e] = product[src * MOST:(src + 1) * MOST]
-        outs.append(pltpu.make_async_copy(out_ref.at[:, e], out_hbm.at[0, :, e], osem.at[3 + e]))
-        outs[-1].start()
+            out_ref[0, src, e] = product[src * MOST:(src + 1) * MOST]
 
     @pl.when(z + 1 < line)
     def _():
@@ -330,7 +312,15 @@
         @pl.when(c >= d)
         def _():
             group_copy(d).wait_send()
-    for copy in outs:
+
+
+def deliver(*refs):
+    count = (len(refs) - 1) // 2
+    sems = refs[-1]
+    copies = [pltpu.make_async_copy(refs[i], refs[count + i], sems.at[i]) for i in range(count)]
+    for copy in copies:
+        copy.start()
+    for copy in copies:
         copy.wait()
 
 
@@ -349,16 +339,13 @@
     line = peers // 2
     dma = pltpu.SemaphoreType.DMA
     hbm = pl.BlockSpec(memory_space=pl.ANY)
-    qg, kg, vg, out = pl.pallas_call(
+    shapes = ((length, keys), (length, keys), (length, values), (1, peers, experts, MOST, hidden))
+    vmem = pl.BlockSpec(memory_space=pltpu.VMEM)
+    held = pl.pallas_call(
         functools.partial(kernel, groups, peers, chunk),
-        out_shape=(
-            jax.ShapeDtypeStruct((length, keys), BF16),
-            jax.ShapeDtypeStruct((length, keys), BF16),
-            jax.ShapeDtypeStruct((length, values), BF16),
-            jax.ShapeDtypeStruct((1, peers, experts, MOST, hidden), BF16),
-        ),
+        out_shape=tuple(pltpu.VMEM(shape, BF16) for shape in shapes),
         in_specs=[hbm] * 10,
-        out_specs=(hbm,) * 4,
+        out_specs=(vmem,) * 4,
         scratch_shapes=[
             pltpu.VMEM((length, keys), BF16),
             pltpu.VMEM((length, keys), BF16),
@@ -374,10 +361,6 @@
             pltpu.VMEM((peers, experts * MOST, tokens), BF16),
             pltpu.VMEM((peers, experts * MOST, 128), F32),
             pltpu.VMEM((experts, peers * MOST, width), BF16),
-            pltpu.VMEM((peers, experts, MOST, hidden), BF16),
-            pltpu.VMEM((length, keys), BF16),
-            pltpu.VMEM((length, keys), BF16),
-            pltpu.VMEM((length, values), BF16),
             pltpu.VMEM((values + 8, keys), F32),
             pltpu.VMEM((max(1, groups - 1), values + 8, keys), F32),
             pltpu.VMEM((values, keys), F32),
@@ -388,7 +371,6 @@
             pltpu.VMEM((count, values, keys), F32),
             dma((8,)),
             dma((experts,)),
-            dma((3 + experts,)),
             dma((peers,)),
             dma((peers,)),
             dma((3,)),
@@ -416,6 +398,13 @@
         routes.T,
         expert_down,
     )
+    qg, kg, vg, out = pl.pallas_call(
+        deliver,
+        out_shape=tuple(jax.ShapeDtypeStruct(shape, BF16) for shape in shapes),
+        in_specs=[vmem] * 4,
+        out_specs=(hbm,) * 4,
+        scratch_shapes=[dma((4,))],
+    )(*held)
     return (
         qg.reshape(length, heads, keys),
         kg.reshape(length, heads, keys),

time: 32.4 us -> 30 us (0.926)
  local copies, waits for them, and re-layouts: 6.29 us -> 2.63 us
  Pallas kernels: 25.2 us -> 26.6 us
    unnamed x4 -> x8, local copies, waits for them, and re-layouts: 6.29 us -> 2.63 us
    pallas_call x0 -> x1, Pallas kernels: none -> 2.04 us  [local(): pl.pallas_call(deliver, out_shape=tuple((jax.ShapeDtypeStruct(shape, BF16...]
    pallas_call x1, Pallas kernels: 25.2 us -> 24.5 us  [local(): pl.pallas_call(functools.partial(kernel, groups, peers, chunk), out_shape...]
where the time goes in v2:
time: 30 us; the launch traced here: 29.9 us
  Pallas kernels  26.6 us (89%)
  local copies, waits for them, and re-layouts  2.63 us (9%)
  between operations  0.65 us (2%)
    pallas_call x1, Pallas kernels, local(): pl.pallas_call(functools.partial(kernel, groups, peers, chunk), out_shape...  24.5 us
    unnamed x8, local copies, waits for them, and re-layouts  2.63 us
    pallas_call x1, Pallas kernels, local(): pl.pallas_call(deliver, out_shape=tuple((jax.ShapeDtypeStruct(shape, BF16...  2.04 us

profile of v2, /device:TPU:1, one launch (start us, length us, event | category | flops | bytes accessed | tf_op | source)
XLA Modules:
  0.0 29.9 jit_solution(2666020008672273933)
XLA Ops:
  0.6 24.5 %shard_map.129 = (bf16[256,128]{1,0:T(8,128)(2,1)S(1)}, bf16[256,128]{1,0:T(8,128)(2,1)S(1)}, bf16[256,128]{1,0:T(8,128)(2,1)S(1)}, bf16[1,8,4,16,512]{4,3,2,1,0:T(8,128)(2,1)S(1)}) custom-call(bf16[256,128]{1,0:T(8,128)(2,1)} %bitcast.11, bf16[256,128]{1,0:T(8,128)(2,1)} %bitcast.12, bf16[256,128]{1,0:T(8,128)(2,1)} %bitcast.13, bf16[256,128]{1,0:T(8,128)(2,1)} %bitcast.14, ...), custom_call_target="tpu_custom_call" | custom-call | flops 1207959552 | bytes 9437184 | tf_op jit(solution)/shard_map/pallas_call | solution.py:344
  25.2 0.0 copy-start
  25.2 0.8 %copy-done = bf16[1,8,4,16,512]{4,3,2,1,0:T(8,128)(2,1)} copy-done((bf16[1,8,4,16,512]{4,3,2,1,0:T(8,128)(2,1)}, bf16[1,8,4,16,512]{4,3,2,1,0:T(8,128)(2,1)S(1)}, u32[]{:S(2)}) %copy-start) | copy-done | bytes 524312
  26.0 0.0 copy-start.1
  26.0 0.6 %copy-done.1 = bf16[256,128]{1,0:T(8,128)(2,1)} copy-done((bf16[256,128]{1,0:T(8,128)(2,1)}, bf16[256,128]{1,0:T(8,128)(2,1)S(1)}, u32[]{:S(2)}) %copy-start.1) | copy-done | bytes 65560
  26.6 0.0 copy-start.2
  26.6 0.6 %copy-done.2 = bf16[256,128]{1,0:T(8,128)(2,1)} copy-done((bf16[256,128]{1,0:T(8,128)(2,1)}, bf16[256,128]{1,0:T(8,128)(2,1)S(1)}, u32[]{:S(2)}) %copy-start.2) | copy-done | bytes 65560
  27.2 0.0 copy-start.3
  27.2 0.6 %copy-done.3 = bf16[256,128]{1,0:T(8,128)(2,1)} copy-done((bf16[256,128]{1,0:T(8,128)(2,1)}, bf16[256,128]{1,0:T(8,128)(2,1)S(1)}, u32[]{:S(2)}) %copy-start.3) | copy-done | bytes 65560
  27.8 2.0 %shard_map.130 = (bf16[256,128]{1,0:T(8,128)(2,1)}, bf16[256,128]{1,0:T(8,128)(2,1)}, bf16[256,128]{1,0:T(8,128)(2,1)}, bf16[1,8,4,16,512]{4,3,2,1,0:T(8,128)(2,1)}) custom-call(bf16[256,128]{1,0:T(8,128)(2,1)} %copy-done.1, bf16[256,128]{1,0:T(8,128)(2,1)} %copy-done.2, bf16[256,128]{1,0:T(8,128)(2,1)} %copy-done.3, bf16[1,8,4,16,512]{4,3,2,1,0:T(8,128)(2,1)} %copy-done), custom_call_target="tpu_custom_call" | custom-call | tf_op jit(solution)/shard_map/pallas_call | solution.py:401
Async XLA Ops:
  25.2 0.8 %copy-start = (bf16[1,8,4,16,512]{4,3,2,1,0:T(8,128)(2,1)}, bf16[1,8,4,16,512]{4,3,2,1,0:T(8,128)(2,1)S(1)}, u32[]{:S(2)}) copy-start(bf16[1,8,4,16,512]{4,3,2,1,0:T(8,128)(2,1)S(1)} %get-tuple-element.15.refs_3_) | copy-start | bytes 1572868
  26.0 0.6 %copy-start.1 = (bf16[256,128]{1,0:T(8,128)(2,1)}, bf16[256,128]{1,0:T(8,128)(2,1)S(1)}, u32[]{:S(2)}) copy-start(bf16[256,128]{1,0:T(8,128)(2,1)S(1)} %get-tuple-element.12.refs_0_) | copy-start | bytes 196612
  26.6 0.6 %copy-start.2 = (bf16[256,128]{1,0:T(8,128)(2,1)}, bf16[256,128]{1,0:T(8,128)(2,1)S(1)}, u32[]{:S(2)}) copy-start(bf16[256,128]{1,0:T(8,128)(2,1)S(1)} %get-tuple-element.13.refs_1_) | copy-start | bytes 196612
  27.2 0.6 %copy-start.3 = (bf16[256,128]{1,0:T(8,128)(2,1)}, bf16[256,128]{1,0:T(8,128)(2,1)S(1)}, u32[]{:S(2)}) copy-start(bf16[256,128]{1,0:T(8,128)(2,1)S(1)} %get-tuple-element.14.refs_2_) | copy-start | bytes 196612

commit v3 on v2

--- a/solution.py
+++ b/solution.py
@@ -33,11 +33,11 @@
 
 
 def kernel(
-    groups, peers, chunk,
+    groups, peers, chunk, parts,
     q_hbm, k_hbm, v_hbm, g_hbm, d_hbm, s_hbm, x_hbm, gate_hbm, route_hbm, w_hbm,
     qg_ref, kg_ref, vg_ref, out_ref,
     q_ref, k_ref, v_ref, g_ref, d_ref, s_ref, gate_ref, route_ref, meta, xall, w_ref,
-    pick, scale, slots, message, arrived, carry, ed_ref, red_ref,
+    pick, scale, slots, sums, message, arrived, carry, ed_ref, red_ref,
     kpart, vpart, mstate, lsem, wsem, msend, mrecv, xown, xlocal, xsend, xrecv, csend, crecv,
 ):
     c = lax.axis_index("ctx")
@@ -48,8 +48,9 @@
     sibling = z * 2 + 1 - h
     length = q_ref.shape[0]
     count = length // chunk
-    experts = w_ref.shape[0]
-    tokens = xall.shape[1]
+    experts = w_ref.shape[1]
+    tokens = x_hbm.shape[0]
+    wide = x_hbm.shape[1] // parts
 
     barrier = pltpu.get_barrier_semaphore()
     for off in range(1, peers):
@@ -66,9 +67,16 @@
     ]
     for load in loads:
         load.start()
-    own = pltpu.make_async_copy(x_hbm, xall.at[s], xlocal)
-    own.start()
-    weights = [pltpu.make_async_copy(w_hbm.at[e], w_ref.at[e], wsem.at[e]) for e in range(experts)]
+    def columns(p):
+        return pl.ds(p * wide, wide)
+
+    def block(p, src):
+        return xall.at[p, pl.ds(pl.multiple_of(src * tokens, tokens), tokens)]
+
+    own = [pltpu.make_async_copy(x_hbm.at[:, columns(p)], block(p, s), xlocal.at[p]) for p in range(parts)]
+    for copy in own:
+        copy.start()
+    weights = [pltpu.make_async_copy(w_hbm.at[:, :, columns(p)], w_ref.at[p], wsem.at[p]) for p in range(parts)]
     for weight in weights:
         weight.start()
     loads[0].wait()
@@ -79,24 +87,32 @@
 
     pl.semaphore_wait(barrier, peers - 1 + groups - 1)
 
-    def send_x(src, dst, slot, sem, to):
+    def send_x(source, p, slot, sem, to):
         return pltpu.make_async_remote_copy(
-            src_ref=src, dst_ref=dst, send_sem=sem, recv_sem=xrecv.at[slot], device_id={"exp": to}, device_id_type=MESH
+            src_ref=source, dst_ref=block(p, slot), send_sem=sem, recv_sem=xrecv.at[p, slot],
+            device_id={"exp": to}, device_id_type=MESH,
         )
 
-    to_right = send_x(x_hbm, xall.at[s], s, xown.at[0], (s + 2) % peers)
-    to_left = send_x(x_hbm, xall.at[s], s, xown.at[1], (s + peers - 2) % peers)
-    to_sibling = send_x(x_hbm, xall.at[s], s, xown.at[2], sibling)
-
-    @pl.when(z + 1 < line)
-    def _():
-        to_right.start()
-
-    @pl.when(z >= 1)
-    def _():
-        to_left.start()
-
-    to_sibling.start()
+    def firsts(p):
+        mine = x_hbm.at[:, columns(p)]
+        return (
+            send_x(mine, p, s, xown.at[p, 0], (s + 2) % peers),
+            send_x(mine, p, s, xown.at[p, 1], (s + peers - 2) % peers),
+            send_x(mine, p, s, xown.at[p, 2], sibling),
+        )
+
+    for p in range(parts):
+        to_right, to_left, to_sibling = firsts(p)
+
+        @pl.when(z + 1 < line)
+        def _():
+            to_right.start()
+
+        @pl.when(z >= 1)
+        def _():
+            to_left.start()
+
+        to_sibling.start()
 
     metas = []
     for off in range(1, peers):
@@ -114,15 +130,16 @@
             (right, z + d < line, (s + peers - 2) % peers, z >= 1),
         )
 
-    def forwards(d, side):
+    def forwards(d, side, p):
         src, valid, onward, goes = ways(d)[side]
-        on = send_x(xall.at[src], xall.at[src], src, xsend.at[(d - 1) * 4 + side * 2], onward)
-        across = send_x(xall.at[src], xall.at[src], src, xsend.at[(d - 1) * 4 + side * 2 + 1], sibling)
+        row = (d - 1) * 4 + side * 2
+        on = send_x(block(p, src), p, src, xsend.at[row, p], onward)
+        across = send_x(block(p, src), p, src, xsend.at[row + 1, p], sibling)
         return src, valid, goes, on, across
 
-    def relay(d):
+    def relay(d, p):
         for side in range(2):
-            src, valid, goes, on, across = forwards(d, side)
+            src, valid, goes, on, across = forwards(d, side, p)
 
             @pl.when(valid)
             def _():
@@ -133,6 +150,16 @@
                     on.start()
 
                 across.start()
+
+    pending = [(d, p) for d in range(1, line) for p in range(parts)]
+
+    def step():
+        if pending:
+            relay(*pending.pop(0))
+
+    def ensure(d, p):
+        while pending and pending[0] <= (d, p):
+            step()
 
     for load in loads[2:]:
         load.wait()
@@ -176,8 +203,59 @@
         def _():
             group_copy(d).start()
 
-    if line > 1:
-        relay(1)
+    before = jnp.where(
+        lax.broadcasted_iota(jnp.int32, (tokens, tokens), 0) < lax.broadcasted_iota(jnp.int32, (tokens, tokens), 1), 1.0, 0.0
+    ).astype(BF16)
+    for off in range(1, peers):
+        src = (s + off) % peers
+        pltpu.make_async_remote_copy(
+            src_ref=meta.at[src], dst_ref=meta.at[src], send_sem=msend.at[0], recv_sem=mrecv.at[src],
+            device_id={"exp": sibling}, device_id_type=MESH,
+        ).wait_recv()
+    gates = meta[:, 0:top]
+    routes = meta[:, top:2 * top]
+    first = (s * experts).astype(F32)
+    place = lax.broadcasted_iota(jnp.int32, (peers, MOST, tokens), 1).astype(F32)
+    pair = 2 * MOST
+    core = lax.broadcasted_iota(jnp.int32, (line, pair, 2 * tokens), 1) // MOST
+    mine = core == lax.broadcasted_iota(jnp.int32, (line, pair, 2 * tokens), 2) // tokens
+    for e in range(experts):
+        hit = routes == first + e
+        member = jnp.sum(jnp.where(hit, 1.0, 0.0), axis=1)
+        gate = jnp.sum(jnp.where(hit, gates, 0.0), axis=1)
+        earlier = jnp.where(member > 0.5, dot(member.astype(BF16), before, 1, 0), -1.0)
+        chosen = jnp.where(earlier[:, None, :] == place, 1.0, 0.0)
+        weight = jnp.sum(chosen * gate[:, None, :], axis=2, keepdims=True).reshape(line, pair, 1)
+        chosen = chosen.reshape(line, pair, tokens)
+        chosen = jnp.where(mine, jnp.concatenate([chosen, chosen], axis=2), 0.0)
+        pick[:, e * pair:(e + 1) * pair, :] = chosen.astype(BF16)
+        scale[:, e * pair:(e + 1) * pair, :] = jnp.broadcast_to(weight, (line, pair, scale.shape[2]))
+
+    def build(p, chip):
+        picked = dot(pick[chip], xall[p, pl.ds(pl.multiple_of(chip * 2 * tokens, 2 * tokens), 2 * tokens), :], 1, 0)
+        scaled = (picked * scale[chip][:, 0:1]).astype(BF16)
+        for e in range(experts):
+            slots[p, e, pl.ds(pl.multiple_of(chip * pair, pair), pair), :] = scaled[e * pair:(e + 1) * pair]
+
+    def arrival(p, src):
+        return send_x(block(p, src), p, src, xown.at[p, 2], sibling)
+
+    def finish(d, p):
+        ensure(d, p)
+        for side in range(2):
+            src, valid, onward, goes = ways(d)[side]
+
+            @pl.when(valid)
+            def _():
+                arrival(p, (src // 2) * 2 + 1 - h).wait_recv()
+                build(p, src // 2)
+
+    step()
+    for p in range(parts):
+        own[p].wait()
+        arrival(p, sibling).wait_recv()
+        build(p, z)
+    step()
 
     state = s_ref[...].T
     for a in range(count):
@@ -192,70 +270,15 @@
         qg_ref[part, :] = (ups[a] * qg).astype(BF16)
         kpart[part, :] = mm(flipped, enlarged[a], 1, 0)
         vpart[part, :] = mm(affinity, [g], 1, 0)
-        if a == 0 and line > 2:
-            relay(2)
+        step()
         if a + 1 < count:
             state = jnp.exp(ends[a]) * state + mm([v], red, 0, 0) * halves[a]
 
-    before = jnp.where(
-        lax.broadcasted_iota(jnp.int32, (tokens, tokens), 0) < lax.broadcasted_iota(jnp.int32, (tokens, tokens), 1), 1.0, 0.0
-    ).astype(BF16)
-
-    for off in range(1, peers):
-        src = (s + off) % peers
-        pltpu.make_async_remote_copy(
-            src_ref=meta.at[src], dst_ref=meta.at[src], send_sem=msend.at[0], recv_sem=mrecv.at[src],
-            device_id={"exp": sibling}, device_id_type=MESH,
-        ).wait_recv()
-    gates = meta[:, 0:top]
-    routes = meta[:, top:2 * top]
-    first = (s * experts).astype(F32)
-    place = lax.broadcasted_iota(jnp.int32, (peers, MOST, tokens), 1).astype(F32)
-    for e in range(experts):
-        hit = routes == first + e
-        member = jnp.sum(jnp.where(hit, 1.0, 0.0), axis=1)
-        gate = jnp.sum(jnp.where(hit, gates, 0.0), axis=1)
-        earlier = jnp.where(member > 0.5, dot(member.astype(BF16), before, 1, 0), -1.0)
-        chosen = jnp.where(earlier[:, None, :] == place, 1.0, 0.0)
-        pick[:, e * MOST:(e + 1) * MOST, :] = chosen.astype(BF16)
-        weight = jnp.sum(chosen * gate[:, None, :], axis=2, keepdims=True)
-        scale[:, e * MOST:(e + 1) * MOST, :] = jnp.broadcast_to(weight, (peers, MOST, scale.shape[2]))
-
-    def build(src):
-        rows_of = dot(pick[src], xall[src], 1, 0)
-        scaled = (rows_of * scale[src][:, 0:1]).astype(BF16)
-        for e in range(experts):
-            slots[e, pl.ds(pl.multiple_of(src * MOST, MOST), MOST), :] = scaled[e * MOST:(e + 1) * MOST]
-
-    own.wait()
-    build(s)
-    send_x(xall.at[sibling], xall.at[sibling], sibling, xown.at[2], sibling).wait_recv()
-    build(sibling)
-
-    def finish(d):
-        def one(i, unused):
-            side = i // 2
-            across = i % 2
-            step = jnp.where(side == 0, peers - 2 * d, 2 * d)
-            valid = jnp.where(side == 0, z >= d, z + d < line)
-            mine = (s + step) % peers
-            other = (mine // 2) * 2 + 1 - h
-            src = jnp.where(across == 0, mine, other)
-
-            @pl.when(valid)
-            def _():
-                @pl.when(across == 1)
-                def _():
-                    send_x(xall.at[src], xall.at[src], src, xown.at[2], sibling).wait_recv()
-
-                build(src)
-
-            return unused
-
-        lax.fori_loop(0, 4, one, 0)
-
-    if line > 1:
-        finish(1)
+    near = min(2, line)
+    for d in range(1, near):
+        for p in range(parts):
+            finish(d, p)
+            step()
 
     carry[...] = jnp.zeros_like(carry)
     for d in reversed(range(1, groups)):
@@ -275,39 +298,48 @@
         if a > 0:
             after = mstate[a] + jnp.exp(ends[a]) * after
 
-    for d in range(2, line):
-        if d > 2:
-            relay(d)
-        finish(d)
-
-    for e in range(experts):
-        weights[e].wait()
-        product = dot(slots[e], w_ref[e], 1, 1).astype(BF16)
-        for src in range(peers):
-            out_ref[0, src, e] = product[src * MOST:(src + 1) * MOST]
-
-    @pl.when(z + 1 < line)
-    def _():
-        to_right.wait_send()
-
-    @pl.when(z >= 1)
-    def _():
-        to_left.wait_send()
-
-    to_sibling.wait_send()
+    for p in range(parts):
+        ensure(line - 1, min(p + 1, parts - 1))
+        for d in range(near, line):
+            finish(d, p)
+        weights[p].wait()
+        for e in range(experts):
+            product = dot(slots[p, e], w_ref[p, e], 1, 1)
+            if p > 0:
+                product = product + sums[e]
+            if p < parts - 1:
+                sums[e] = product
+            else:
+                product = product.astype(BF16)
+                for src in range(peers):
+                    out_ref[0, src, e] = product[src * MOST:(src + 1) * MOST]
+
+    for p in range(parts):
+        to_right, to_left, to_sibling = firsts(p)
+
+        @pl.when(z + 1 < line)
+        def _():
+            to_right.wait_send()
+
+        @pl.when(z >= 1)
+        def _():
+            to_left.wait_send()
+
+        to_sibling.wait_send()
     for copy in metas:
         copy.wait_send()
     for d in range(1, line):
-        for side in range(2):
-            src, valid, goes, on, across = forwards(d, side)
-
-            @pl.when(valid)
-            def _():
-                @pl.when(goes)
+        for p in range(parts):
+            for side in range(2):
+                src, valid, goes, on, across = forwards(d, side, p)
+
+                @pl.when(valid)
                 def _():
-                    on.wait_send()
-
-                across.wait_send()
+                    @pl.when(goes)
+                    def _():
+                        on.wait_send()
+
+                    across.wait_send()
     for d in range(1, groups):
         @pl.when(c >= d)
         def _():
@@ -337,12 +369,13 @@
     chunk = min(128, length)
     count = length // chunk
     line = peers // 2
+    parts = 3 if width % 384 == 0 else 1
     dma = pltpu.SemaphoreType.DMA
     hbm = pl.BlockSpec(memory_space=pl.ANY)
     shapes = ((length, keys), (length, keys), (length, values), (1, peers, experts, MOST, hidden))
     vmem = pl.BlockSpec(memory_space=pltpu.VMEM)
     held = pl.pallas_call(
-        functools.partial(kernel, groups, peers, chunk),
+        functools.partial(kernel, groups, peers, chunk, parts),
         out_shape=tuple(pltpu.VMEM(shape, BF16) for shape in shapes),
         in_specs=[hbm] * 10,
         out_specs=(vmem,) * 4,
@@ -356,11 +389,12 @@
             pltpu.VMEM((top, tokens), F32),
             pltpu.VMEM((top, tokens), jnp.int32),
             pltpu.VMEM((peers, 2 * top, tokens), F32),
-            pltpu.VMEM((peers, tokens, width), BF16),
-            pltpu.VMEM((experts, hidden, width), BF16),
-            pltpu.VMEM((peers, experts * MOST, tokens), BF16),
-            pltpu.VMEM((peers, experts * MOST, 128), F32),
-            pltpu.VMEM((experts, peers * MOST, width), BF16),
+            pltpu.VMEM((parts, peers * tokens, width // parts), BF16),
+            pltpu.VMEM((parts, experts, hidden, width // parts), BF16),
+            pltpu.VMEM((line, 2 * experts * MOST, 2 * tokens), BF16),
+            pltpu.VMEM((line, 2 * experts * MOST, 128), F32),
+            pltpu.VMEM((parts, experts, peers * MOST, width // parts), BF16),
+            pltpu.VMEM((experts, peers * MOST, hidden), F32),
             pltpu.VMEM((values + 8, keys), F32),
             pltpu.VMEM((max(1, groups - 1), values + 8, keys), F32),
             pltpu.VMEM((values, keys), F32),
@@ -370,13 +404,13 @@
             pltpu.VMEM((length, values), F32),
             pltpu.VMEM((count, values, keys), F32),
             dma((8,)),
-            dma((experts,)),
+            dma((parts,)),
             dma((peers,)),
             dma((peers,)),
-            dma((3,)),
-            dma,
-            dma((max(1, line - 1) * 4,)),
-            dma((peers,)),
+            dma((parts, 3)),
+            dma((parts,)),
+            dma((max(1, line - 1) * 4, parts)),
+            dma((parts, peers)),
             dma((max(1, groups - 1),)),
             dma((max(1, groups - 1),)),
         ],
@@ -404,6 +438,7 @@
         in_specs=[vmem] * 4,
         out_specs=(hbm,) * 4,
         scratch_shapes=[dma((4,))],
+        compiler_params=pltpu.CompilerParams(vmem_limit_bytes=1024 * 1024),
     )(*held)
     return (
         qg.reshape(length, heads, keys),

time: 30 us -> 27.5 us (0.917)
  the two profiles are of different devices: /device:TPU:1 before, /device:TPU:0 now
where the time goes in v3:
time: 27.5 us; the launch traced here: 27.3 us
  Pallas kernels  26.7 us (97%)
  between operations  0.64 us (2%)
    pallas_call x1, Pallas kernels, local(): pl.pallas_call(functools.partial(kernel, groups, peers, chunk, parts), ou...  25.8 us
    pallas_call x1, Pallas kernels, local(): pl.pallas_call(deliver, out_shape=tuple((jax.ShapeDtypeStruct(shape, BF16...  0.9 us

profile of v3, /device:TPU:0, one launch (start us, length us, event | category | flops | bytes accessed | tf_op | source)
XLA Modules:
  0.0 27.3 jit_solution(6900280299786158138)
XLA Ops:
  0.6 25.8 %shard_map.129 = (bf16[256,128]{1,0:T(8,128)(2,1)S(1)}, bf16[256,128]{1,0:T(8,128)(2,1)S(1)}, bf16[256,128]{1,0:T(8,128)(2,1)S(1)}, bf16[1,8,4,16,512]{4,3,2,1,0:T(8,128)(2,1)S(1)}) custom-call(bf16[256,128]{1,0:T(8,128)(2,1)} %bitcast.11, bf16[256,128]{1,0:T(8,128)(2,1)} %bitcast.12, bf16[256,128]{1,0:T(8,128)(2,1)} %bitcast.13, bf16[256,128]{1,0:T(8,128)(2,1)} %bitcast.14, ...), custom_call_target="tpu_custom_call" | custom-call | flops 1207959552 | bytes 9437184 | tf_op jit(solution)/shard_map/pallas_call | solution.py:377
  26.4 0.9 %shard_map.130 = (bf16[256,128]{1,0:T(8,128)(2,1)}, bf16[256,128]{1,0:T(8,128)(2,1)}, bf16[256,128]{1,0:T(8,128)(2,1)}, bf16[1,8,4,16,512]{4,3,2,1,0:T(8,128)(2,1)}) custom-call(bf16[256,128]{1,0:T(8,128)(2,1)S(1)} %get-tuple-element.12.refs_0_, bf16[256,128]{1,0:T(8,128)(2,1)S(1)} %get-tuple-element.13.refs_1_, ...), custom_call_target="tpu_custom_call" | custom-call | tf_op jit(solution)/shard_map/pallas_call | solution.py:435

commit v4 on v3

--- a/solution.py
+++ b/solution.py
@@ -93,26 +93,28 @@
             device_id={"exp": to}, device_id_type=MESH,
         )
 
-    def firsts(p):
+    def ways(d):
+        return ((s + peers - 2 * d) % peers, z >= d), ((s + 2 * d) % peers, z + d < line)
+
+    def outgoing(p):
         mine = x_hbm.at[:, columns(p)]
-        return (
-            send_x(mine, p, s, xown.at[p, 0], (s + 2) % peers),
-            send_x(mine, p, s, xown.at[p, 1], (s + peers - 2) % peers),
-            send_x(mine, p, s, xown.at[p, 2], sibling),
-        )
-
+        for d in reversed(range(1, line)):
+            for side, (to, valid) in enumerate(ways(d)):
+                yield valid, send_x(mine, p, s, xsend.at[(d - 1) * 4 + side * 2, p], to)
+
+    def incoming(p):
+        for d in range(1, line):
+            for side, (src, valid) in enumerate(ways(d)):
+                yield src, valid, send_x(block(p, src), p, src, xsend.at[(d - 1) * 4 + side * 2 + 1, p], sibling)
+
+    beside = [send_x(x_hbm.at[:, columns(p)], p, s, xown.at[p], sibling) for p in range(parts)]
     for p in range(parts):
-        to_right, to_left, to_sibling = firsts(p)
-
-        @pl.when(z + 1 < line)
-        def _():
-            to_right.start()
-
-        @pl.when(z >= 1)
-        def _():
-            to_left.start()
-
-        to_sibling.start()
+        for valid, copy in outgoing(p):
+            @pl.when(valid)
+            def _():
+                copy.start()
+
+        beside[p].start()
 
     metas = []
     for off in range(1, peers):
@@ -122,44 +124,12 @@
         ))
         metas[-1].start()
 
-    def ways(d):
-        left = (s + peers - 2 * d) % peers
-        right = (s + 2 * d) % peers
-        return (
-            (left, z >= d, (s + 2) % peers, z + 1 < line),
-            (right, z + d < line, (s + peers - 2) % peers, z >= 1),
-        )
-
-    def forwards(d, side, p):
-        src, valid, onward, goes = ways(d)[side]
-        row = (d - 1) * 4 + side * 2
-        on = send_x(block(p, src), p, src, xsend.at[row, p], onward)
-        across = send_x(block(p, src), p, src, xsend.at[row + 1, p], sibling)
-        return src, valid, goes, on, across
-
-    def relay(d, p):
-        for side in range(2):
-            src, valid, goes, on, across = forwards(d, side, p)
-
+    def relay(p):
+        for src, valid, copy in incoming(p):
             @pl.when(valid)
             def _():
-                across.wait_recv()
-
-                @pl.when(goes)
-                def _():
-                    on.start()
-
-                across.start()
-
-    pending = [(d, p) for d in range(1, line) for p in range(parts)]
-
-    def step():
-        if pending:
-            relay(*pending.pop(0))
-
-    def ensure(d, p):
-        while pending and pending[0] <= (d, p):
-            step()
+                copy.wait_recv()
+                copy.start()
 
     for load in loads[2:]:
         load.wait()
@@ -238,27 +208,34 @@
             slots[p, e, pl.ds(pl.multiple_of(chip * pair, pair), pair), :] = scaled[e * pair:(e + 1) * pair]
 
     def arrival(p, src):
-        return send_x(block(p, src), p, src, xown.at[p, 2], sibling)
-
-    def finish(d, p):
-        ensure(d, p)
-        for side in range(2):
-            src, valid, onward, goes = ways(d)[side]
-
+        return send_x(block(p, src), p, src, xown.at[p], sibling)
+
+    def finish(p):
+        for src, valid in [way for d in range(1, line) for way in ways(d)]:
             @pl.when(valid)
             def _():
                 arrival(p, (src // 2) * 2 + 1 - h).wait_recv()
                 build(p, src // 2)
 
-    step()
+    def multiply(p):
+        weights[p].wait()
+        for e in range(experts):
+            product = dot(w_ref[p, e], slots[p, e], 1, 1)
+            if p > 0:
+                product = product + sums[e]
+            if p < parts - 1:
+                sums[e] = product
+            else:
+                product = product.T.astype(BF16)
+                for src in range(peers):
+                    out_ref[0, src, e] = product[src * MOST:(src + 1) * MOST]
+
     for p in range(parts):
         own[p].wait()
         arrival(p, sibling).wait_recv()
         build(p, z)
-    step()
-
-    state = s_ref[...].T
-    for a in range(count):
+
+    def attend(a, state):
         part = pl.ds(a * chunk, chunk)
         g = g_ref[part, :]
         v = v_ref[part, :]
@@ -270,76 +247,54 @@
         qg_ref[part, :] = (ups[a] * qg).astype(BF16)
         kpart[part, :] = mm(flipped, enlarged[a], 1, 0)
         vpart[part, :] = mm(affinity, [g], 1, 0)
-        step()
         if a + 1 < count:
             state = jnp.exp(ends[a]) * state + mm([v], red, 0, 0) * halves[a]
-
-    near = min(2, line)
-    for d in range(1, near):
-        for p in range(parts):
-            finish(d, p)
-            step()
-
-    carry[...] = jnp.zeros_like(carry)
-    for d in reversed(range(1, groups)):
-        @pl.when(c + d < groups)
-        def _():
-            group_copy(d).wait_recv()
-            size = carry.shape[0]
-            carry[...] = arrived[d - 1, 0:size, :] + arrived[d - 1, size:size + 1, :] * carry[...]
-    after = carry[...]
-    for a in reversed(range(count)):
-        part = pl.ds(a * chunk, chunk)
-        later = split(after * halves[a])
-        kg = kpart[part, :] + mm([v_ref[part, :]], later, 1, 0)
-        kg_ref[part, :] = (ed_ref[part, :] * kg).astype(BF16)
-        vg = vpart[part, :] + mm(split(red_ref[part, :]), later, 1, 1)
-        vg_ref[part, :] = vg.astype(BF16)
-        if a > 0:
-            after = mstate[a] + jnp.exp(ends[a]) * after
-
+        return state
+
+    def adjoin():
+        carry[...] = jnp.zeros_like(carry)
+        for d in reversed(range(1, groups)):
+            @pl.when(c + d < groups)
+            def _():
+                group_copy(d).wait_recv()
+                size = carry.shape[0]
+                carry[...] = arrived[d - 1, 0:size, :] + arrived[d - 1, size:size + 1, :] * carry[...]
+        after = carry[...]
+        for a in reversed(range(count)):
+            part = pl.ds(a * chunk, chunk)
+            later = split(after * halves[a])
+            kg = kpart[part, :] + mm([v_ref[part, :]], later, 1, 0)
+            kg_ref[part, :] = (ed_ref[part, :] * kg).astype(BF16)
+            vg = vpart[part, :] + mm(split(red_ref[part, :]), later, 1, 1)
+            vg_ref[part, :] = vg.astype(BF16)
+            if a > 0:
+                after = mstate[a] + jnp.exp(ends[a]) * after
+
+    state = s_ref[...].T
+    turn = 0
     for p in range(parts):
-        ensure(line - 1, min(p + 1, parts - 1))
-        for d in range(near, line):
-            finish(d, p)
-        weights[p].wait()
-        for e in range(experts):
-            product = dot(slots[p, e], w_ref[p, e], 1, 1)
-            if p > 0:
-                product = product + sums[e]
-            if p < parts - 1:
-                sums[e] = product
-            else:
-                product = product.astype(BF16)
-                for src in range(peers):
-                    out_ref[0, src, e] = product[src * MOST:(src + 1) * MOST]
+        relay(p)
+        while turn < count and (turn <= p or p == parts - 1):
+            state = attend(turn, state)
+            turn += 1
+        if p == parts - 1:
+            adjoin()
+        finish(p)
+        multiply(p)
 
     for p in range(parts):
-        to_right, to_left, to_sibling = firsts(p)
-
-        @pl.when(z + 1 < line)
-        def _():
-            to_right.wait_send()
-
-        @pl.when(z >= 1)
-        def _():
-            to_left.wait_send()
-
-        to_sibling.wait_send()
+        for valid, copy in outgoing(p):
+            @pl.when(valid)
+            def _():
+                copy.wait_send()
+
+        beside[p].wait_send()
+        for src, valid, copy in incoming(p):
+            @pl.when(valid)
+            def _():
+                copy.wait_send()
     for copy in metas:
         copy.wait_send()
-    for d in range(1, line):
-        for p in range(parts):
-            for side in range(2):
-                src, valid, goes, on, across = forwards(d, side, p)
-
-                @pl.when(valid)
-                def _():
-                    @pl.when(goes)
-                    def _():
-                        on.wait_send()
-
-                    across.wait_send()
     for d in range(1, groups):
         @pl.when(c >= d)
         def _():
@@ -394,7 +349,7 @@
             pltpu.VMEM((line, 2 * experts * MOST, 2 * tokens), BF16),
             pltpu.VMEM((line, 2 * experts * MOST, 128), F32),
             pltpu.VMEM((parts, experts, peers * MOST, width // parts), BF16),
-            pltpu.VMEM((experts, peers * MOST, hidden), F32),
+            pltpu.VMEM((experts, hidden, peers * MOST), F32),
             pltpu.VMEM((values + 8, keys), F32),
             pltpu.VMEM((max(1, groups - 1), values + 8, keys), F32),
             pltpu.VMEM((values, keys), F32),
@@ -407,7 +362,7 @@
             dma((parts,)),
             dma((peers,)),
             dma((peers,)),
-            dma((parts, 3)),
+            dma((parts,)),
             dma((parts,)),
             dma((max(1, line - 1) * 4, parts)),
             dma((parts, peers)),

time: 27.5 us -> 32.5 us (1.18)
  Pallas kernels: 26.7 us -> 31.7 us
    pallas_call x1, Pallas kernels: 25.8 us -> 30.8 us  [local(): pl.pallas_call(functools.partial(kernel, groups, peers, chunk, parts), ou...]
where the time goes in v4:
time: 32.5 us; the launch traced here: 32.3 us
  Pallas kernels  31.7 us (98%)
  between operations  0.64 us (2%)
    pallas_call x1, Pallas kernels, local(): pl.pallas_call(functools.partial(kernel, groups, peers, chunk, parts), ou...  30.8 us
    pallas_call x1, Pallas kernels, local(): pl.pallas_call(deliver, out_shape=tuple((jax.ShapeDtypeStruct(shape, BF16...  0.9 us

profile of v4, /device:TPU:0, one launch (start us, length us, event | category | flops | bytes accessed | tf_op | source)
XLA Modules:
  0.0 32.3 jit_solution(6990069591378159716)
XLA Ops:
  0.6 30.8 %shard_map.129 = (bf16[256,128]{1,0:T(8,128)(2,1)S(1)}, bf16[256,128]{1,0:T(8,128)(2,1)S(1)}, bf16[256,128]{1,0:T(8,128)(2,1)S(1)}, bf16[1,8,4,16,512]{4,3,2,1,0:T(8,128)(2,1)S(1)}) custom-call(bf16[256,128]{1,0:T(8,128)(2,1)} %bitcast.11, bf16[256,128]{1,0:T(8,128)(2,1)} %bitcast.12, bf16[256,128]{1,0:T(8,128)(2,1)} %bitcast.13, bf16[256,128]{1,0:T(8,128)(2,1)} %bitcast.14, ...), custom_call_target="tpu_custom_call" | custom-call | flops 1207959552 | bytes 9437184 | tf_op jit(solution)/shard_map/pallas_call | solution.py:332
  31.4 0.9 %shard_map.130 = (bf16[256,128]{1,0:T(8,128)(2,1)}, bf16[256,128]{1,0:T(8,128)(2,1)}, bf16[256,128]{1,0:T(8,128)(2,1)}, bf16[1,8,4,16,512]{4,3,2,1,0:T(8,128)(2,1)}) custom-call(bf16[256,128]{1,0:T(8,128)(2,1)S(1)} %get-tuple-element.12.refs_0_, bf16[256,128]{1,0:T(8,128)(2,1)S(1)} %get-tuple-element.13.refs_1_, ...), custom_call_target="tpu_custom_call" | custom-call | tf_op jit(solution)/shard_map/pallas_call | solution.py:390

commit v5 on v3

--- a/solution.py
+++ b/solution.py
@@ -250,15 +250,7 @@
                 arrival(p, (src // 2) * 2 + 1 - h).wait_recv()
                 build(p, src // 2)
 
-    step()
-    for p in range(parts):
-        own[p].wait()
-        arrival(p, sibling).wait_recv()
-        build(p, z)
-    step()
-
-    state = s_ref[...].T
-    for a in range(count):
+    def attend(a, state):
         part = pl.ds(a * chunk, chunk)
         g = g_ref[part, :]
         v = v_ref[part, :]
@@ -270,38 +262,30 @@
         qg_ref[part, :] = (ups[a] * qg).astype(BF16)
         kpart[part, :] = mm(flipped, enlarged[a], 1, 0)
         vpart[part, :] = mm(affinity, [g], 1, 0)
-        step()
         if a + 1 < count:
             state = jnp.exp(ends[a]) * state + mm([v], red, 0, 0) * halves[a]
-
-    near = min(2, line)
-    for d in range(1, near):
-        for p in range(parts):
-            finish(d, p)
-            step()
-
-    carry[...] = jnp.zeros_like(carry)
-    for d in reversed(range(1, groups)):
-        @pl.when(c + d < groups)
-        def _():
-            group_copy(d).wait_recv()
-            size = carry.shape[0]
-            carry[...] = arrived[d - 1, 0:size, :] + arrived[d - 1, size:size + 1, :] * carry[...]
-    after = carry[...]
-    for a in reversed(range(count)):
-        part = pl.ds(a * chunk, chunk)
-        later = split(after * halves[a])
-        kg = kpart[part, :] + mm([v_ref[part, :]], later, 1, 0)
-        kg_ref[part, :] = (ed_ref[part, :] * kg).astype(BF16)
-        vg = vpart[part, :] + mm(split(red_ref[part, :]), later, 1, 1)
-        vg_ref[part, :] = vg.astype(BF16)
-        if a > 0:
-            after = mstate[a] + jnp.exp(ends[a]) * after
-
-    for p in range(parts):
-        ensure(line - 1, min(p + 1, parts - 1))
-        for d in range(near, line):
-            finish(d, p)
+        return state
+
+    def adjoin():
+        carry[...] = jnp.zeros_like(carry)
+        for d in reversed(range(1, groups)):
+            @pl.when(c + d < groups)
+            def _():
+                group_copy(d).wait_recv()
+                size = carry.shape[0]
+                carry[...] = arrived[d - 1, 0:size, :] + arrived[d - 1, size:size + 1, :] * carry[...]
+        after = carry[...]
+        for a in reversed(range(count)):
+            part = pl.ds(a * chunk, chunk)
+            later = split(after * halves[a])
+            kg = kpart[part, :] + mm([v_ref[part, :]], later, 1, 0)
+            kg_ref[part, :] = (ed_ref[part, :] * kg).astype(BF16)
+            vg = vpart[part, :] + mm(split(red_ref[part, :]), later, 1, 1)
+            vg_ref[part, :] = vg.astype(BF16)
+            if a > 0:
+                after = mstate[a] + jnp.exp(ends[a]) * after
+
+    def multiply(p):
         weights[p].wait()
         for e in range(experts):
             product = dot(slots[p, e], w_ref[p, e], 1, 1)
@@ -313,6 +297,36 @@
                 product = product.astype(BF16)
                 for src in range(peers):
                     out_ref[0, src, e] = product[src * MOST:(src + 1) * MOST]
+
+    last = line - 1
+    for p in range(parts):
+        own[p].wait()
+        arrival(p, sibling).wait_recv()
+        build(p, z)
+    state = s_ref[...].T
+    done = 0
+    for d in range(1, last):
+        ensure(d, parts - 1)
+        if done < count:
+            state = attend(done, state)
+            done += 1
+        if d + 1 < last:
+            for p in range(parts):
+                finish(d, p)
+    while done < count:
+        state = attend(done, state)
+        done += 1
+    step()
+    if last > 1:
+        for p in range(parts):
+            finish(last - 1, p)
+    step()
+    adjoin()
+    for p in range(parts):
+        if last > 0:
+            finish(last, p)
+        multiply(p)
+        step()
 
     for p in range(parts):
         to_right, to_left, to_sibling = firsts(p)

time: 27.5 us -> 27.8 us (1.011)
  Pallas kernels: 26.7 us -> 27 us
    pallas_call x1, Pallas kernels: 25.8 us -> 26.1 us  [local(): pl.pallas_call(functools.partial(kernel, groups, peers, chunk, parts), ou...]
where the time goes in v5:
time: 27.8 us; the launch traced here: 27.7 us
  Pallas kernels  27 us (97%)
  between operations  0.64 us (2%)
    pallas_call x1, Pallas kernels, local(): pl.pallas_call(functools.partial(kernel, groups, peers, chunk, parts), ou...  26.1 us
    pallas_call x1, Pallas kernels, local(): pl.pallas_call(deliver, out_shape=tuple((jax.ShapeDtypeStruct(shape, BF16...  0.9 us

profile of v5, /device:TPU:0, one launch (start us, length us, event | category | flops | bytes accessed | tf_op | source)
XLA Modules:
  0.0 27.7 jit_solution(5167090193121985106)
XLA Ops:
  0.6 26.1 %shard_map.129 = (bf16[256,128]{1,0:T(8,128)(2,1)S(1)}, bf16[256,128]{1,0:T(8,128)(2,1)S(1)}, bf16[256,128]{1,0:T(8,128)(2,1)S(1)}, bf16[1,8,4,16,512]{4,3,2,1,0:T(8,128)(2,1)S(1)}) custom-call(bf16[256,128]{1,0:T(8,128)(2,1)} %bitcast.11, bf16[256,128]{1,0:T(8,128)(2,1)} %bitcast.12, bf16[256,128]{1,0:T(8,128)(2,1)} %bitcast.13, bf16[256,128]{1,0:T(8,128)(2,1)} %bitcast.14, ...), custom_call_target="tpu_custom_call" | custom-call | flops 1207959552 | bytes 9437184 | tf_op jit(solution)/shard_map/pallas_call | solution.py:391
  26.8 0.9 %shard_map.130 = (bf16[256,128]{1,0:T(8,128)(2,1)}, bf16[256,128]{1,0:T(8,128)(2,1)}, bf16[256,128]{1,0:T(8,128)(2,1)}, bf16[1,8,4,16,512]{4,3,2,1,0:T(8,128)(2,1)}) custom-call(bf16[256,128]{1,0:T(8,128)(2,1)S(1)} %get-tuple-element.12.refs_0_, bf16[256,128]{1,0:T(8,128)(2,1)S(1)} %get-tuple-element.13.refs_1_, ...), custom_call_target="tpu_custom_call" | custom-call | tf_op jit(solution)/shard_map/pallas_call | solution.py:449

commit v6 on v5

--- a/solution.py
+++ b/solution.py
@@ -65,8 +65,6 @@
             (k_hbm, k_ref), (v_hbm, v_ref), (s_hbm, s_ref),
         ])
     ]
-    for load in loads:
-        load.start()
     def columns(p):
         return pl.ds(p * wide, wide)
 
@@ -76,9 +74,9 @@
     own = [pltpu.make_async_copy(x_hbm.at[:, columns(p)], block(p, s), xlocal.at[p]) for p in range(parts)]
     for copy in own:
         copy.start()
+    for load in loads:
+        load.start()
     weights = [pltpu.make_async_copy(w_hbm.at[:, :, columns(p)], w_ref.at[p], wsem.at[p]) for p in range(parts)]
-    for weight in weights:
-        weight.start()
     loads[0].wait()
     loads[1].wait()
     top = gate_ref.shape[0]
@@ -94,7 +92,7 @@
         )
 
     def firsts(p):
-        mine = x_hbm.at[:, columns(p)]
+        mine = block(p, s)
         return (
             send_x(mine, p, s, xown.at[p, 0], (s + 2) % peers),
             send_x(mine, p, s, xown.at[p, 1], (s + peers - 2) % peers),
@@ -102,6 +100,7 @@
         )
 
     for p in range(parts):
+        own[p].wait()
         to_right, to_left, to_sibling = firsts(p)
 
         @pl.when(z + 1 < line)
@@ -121,6 +120,8 @@
             device_id={"exp": (s + off) % peers}, device_id_type=MESH,
         ))
         metas[-1].start()
+    for weight in weights:
+        weight.start()
 
     def ways(d):
         left = (s + peers - 2 * d) % peers
@@ -300,7 +301,6 @@
 
     last = line - 1
     for p in range(parts):
-        own[p].wait()
         arrival(p, sibling).wait_recv()
         build(p, z)
     state = s_ref[...].T
@@ -316,7 +316,6 @@
     while done < count:
         state = attend(done, state)
         done += 1
-    step()
     if last > 1:
         for p in range(parts):
             finish(last - 1, p)
@@ -383,7 +382,7 @@
     chunk = min(128, length)
     count = length // chunk
     line = peers // 2
-    parts = 3 if width % 384 == 0 else 1
+    parts = 1
     dma = pltpu.SemaphoreType.DMA
     hbm = pl.BlockSpec(memory_space=pl.ANY)
     shapes = ((length, keys), (length, keys), (length, values), (1, peers, experts, MOST, hidden))

time: 27.8 us -> 28.7 us (1.032)
  the two profiles are of different devices: /device:TPU:0 before, /device:TPU:1 now
where the time goes in v6:
time: 28.7 us; the launch traced here: 28.5 us
  Pallas kernels  27.8 us (97%)
  between operations  0.64 us (2%)
    pallas_call x1, Pallas kernels, local(): pl.pallas_call(functools.partial(kernel, groups, peers, chunk, parts), ou...  26.9 us
    pallas_call x1, Pallas kernels, local(): pl.pallas_call(deliver, out_shape=tuple((jax.ShapeDtypeStruct(shape, BF16...  0.9 us

profile of v6, /device:TPU:1, one launch (start us, length us, event | category | flops | bytes accessed | tf_op | source)
XLA Modules:
  0.0 28.5 jit_solution(11228743823638332677)
XLA Ops:
  0.6 26.9 %shard_map.129 = (bf16[256,128]{1,0:T(8,128)(2,1)S(1)}, bf16[256,128]{1,0:T(8,128)(2,1)S(1)}, bf16[256,128]{1,0:T(8,128)(2,1)S(1)}, bf16[1,8,4,16,512]{4,3,2,1,0:T(8,128)(2,1)S(1)}) custom-call(bf16[256,128]{1,0:T(8,128)(2,1)} %bitcast.11, bf16[256,128]{1,0:T(8,128)(2,1)} %bitcast.12, bf16[256,128]{1,0:T(8,128)(2,1)} %bitcast.13, bf16[256,128]{1,0:T(8,128)(2,1)} %bitcast.14, ...), custom_call_target="tpu_custom_call" | custom-call | flops 1207959552 | bytes 9437184 | tf_op jit(solution)/shard_map/pallas_call | solution.py:390
  27.6 0.9 %shard_map.130 = (bf16[256,128]{1,0:T(8,128)(2,1)}, bf16[256,128]{1,0:T(8,128)(2,1)}, bf16[256,128]{1,0:T(8,128)(2,1)}, bf16[1,8,4,16,512]{4,3,2,1,0:T(8,128)(2,1)}) custom-call(bf16[256,128]{1,0:T(8,128)(2,1)S(1)} %get-tuple-element.12.refs_0_, bf16[256,128]{1,0:T(8,128)(2,1)S(1)} %get-tuple-element.13.refs_1_, ...), custom_call_target="tpu_custom_call" | custom-call | tf_op jit(solution)/shard_map/pallas_call | solution.py:448

commit v7 on v5

--- a/solution.py
+++ b/solution.py
@@ -77,8 +77,6 @@
     for copy in own:
         copy.start()
     weights = [pltpu.make_async_copy(w_hbm.at[:, :, columns(p)], w_ref.at[p], wsem.at[p]) for p in range(parts)]
-    for weight in weights:
-        weight.start()
     loads[0].wait()
     loads[1].wait()
     top = gate_ref.shape[0]
@@ -121,6 +119,8 @@
             device_id={"exp": (s + off) % peers}, device_id_type=MESH,
         ))
         metas[-1].start()
+    for weight in weights:
+        weight.start()
 
     def ways(d):
         left = (s + peers - 2 * d) % peers
@@ -305,14 +305,19 @@
         build(p, z)
     state = s_ref[...].T
     done = 0
-    for d in range(1, last):
+    if last > 0:
+        ensure(1, parts - 1)
+    state = attend(0, state)
+    done = 1
+    for d in range(2, last):
+        ensure(d, parts - 2)
+        for p in range(parts - 1):
+            finish(d - 1, p)
         ensure(d, parts - 1)
         if done < count:
             state = attend(done, state)
             done += 1
-        if d + 1 < last:
-            for p in range(parts):
-                finish(d, p)
+        finish(d - 1, parts - 1)
     while done < count:
         state = attend(done, state)
         done += 1
@@ -320,13 +325,13 @@
     if last > 1:
         for p in range(parts):
             finish(last - 1, p)
-    step()
+            if p > 0:
+                step()
     adjoin()
     for p in range(parts):
         if last > 0:
             finish(last, p)
         multiply(p)
-        step()
 
     for p in range(parts):
         to_right, to_left, to_sibling = firsts(p)

time: 27.8 us -> 28.4 us (1.022)
  Pallas kernels: 27 us -> 27.6 us
    pallas_call x1, Pallas kernels: 26.1 us -> 26.7 us  [local(): pl.pallas_call(functools.partial(kernel, groups, peers, chunk, parts), ou...]
where the time goes in v7:
time: 28.4 us; the launch traced here: 28.3 us
  Pallas kernels  27.6 us (97%)
  between operations  0.64 us (2%)
    pallas_call x1, Pallas kernels, local(): pl.pallas_call(functools.partial(kernel, groups, peers, chunk, parts), ou...  26.7 us
    pallas_call x1, Pallas kernels, local(): pl.pallas_call(deliver, out_shape=tuple((jax.ShapeDtypeStruct(shape, BF16...  0.9 us

profile of v7, /device:TPU:0, one launch (start us, length us, event | category | flops | bytes accessed | tf_op | source)
XLA Modules:
  0.0 28.3 jit_solution(2297952818181754764)
XLA Ops:
  0.6 26.7 %shard_map.129 = (bf16[256,128]{1,0:T(8,128)(2,1)S(1)}, bf16[256,128]{1,0:T(8,128)(2,1)S(1)}, bf16[256,128]{1,0:T(8,128)(2,1)S(1)}, bf16[1,8,4,16,512]{4,3,2,1,0:T(8,128)(2,1)S(1)}) custom-call(bf16[256,128]{1,0:T(8,128)(2,1)} %bitcast.11, bf16[256,128]{1,0:T(8,128)(2,1)} %bitcast.12, bf16[256,128]{1,0:T(8,128)(2,1)} %bitcast.13, bf16[256,128]{1,0:T(8,128)(2,1)} %bitcast.14, ...), custom_call_target="tpu_custom_call" | custom-call | flops 1207959552 | bytes 9437184 | tf_op jit(solution)/shard_map/pallas_call | solution.py:396
  27.4 0.9 %shard_map.130 = (bf16[256,128]{1,0:T(8,128)(2,1)}, bf16[256,128]{1,0:T(8,128)(2,1)}, bf16[256,128]{1,0:T(8,128)(2,1)}, bf16[1,8,4,16,512]{4,3,2,1,0:T(8,128)(2,1)}) custom-call(bf16[256,128]{1,0:T(8,128)(2,1)S(1)} %get-tuple-element.12.refs_0_, bf16[256,128]{1,0:T(8,128)(2,1)S(1)} %get-tuple-element.13.refs_1_, ...), custom_call_target="tpu_custom_call" | custom-call | tf_op jit(solution)/shard_map/pallas_call | solution.py:454
